TPU v7x, 32 devices: a whole 2x2x4 slice. The times are simulated.
32 devices in a mesh: groups: 2 (over x), expert: 16 (over z, y, core).
Axes of the slice: x: 2, y: 2, z: 4, core: 2. Of those that a mesh axis runs over, the one named last changes fastest.
Arguments:
- tokens: bfloat16 [2048, 2048], P(('groups', 'expert')), parts along dimension 0, may hold values from -6 to 6
- expert_ids: int32 [2048, 8], P(('groups', 'expert')), parts along dimension 0, may hold values from 0 to 15, as said below
- gate_weights: float32 [2048, 8], P(('groups', 'expert')), parts along dimension 0, may hold values from 0.05 to 0.5
- w_gate: bfloat16 [16, 2048, 768], P('expert'), may hold values from -0.125 to 0.125
- w_up: bfloat16 [16, 2048, 768], P('expert'), may hold values from -0.125 to 0.125
- w_down: bfloat16 [16, 768, 2048], P('expert'), may hold values from -0.21875 to 0.21875
Outputs:
- mixed: bfloat16 [2048, 2048], P(('groups', 'expert')), parts along dimension 0
There are 2 independent parts, one for each index of `groups`. A program takes and returns all parts, laid end to end along the dimension named above; an argument that names none is the same for every part. Nothing has to cross between parts.
Inputs may be any that keep to these rules, and one draw needn't show every extreme that they name: `expert_ids`: each token names 8 different experts. Exactly 2 experts are named exactly 64 times by the tokens of every device; every other expert is named at most 28 times by the tokens of one device, and in every draw some such expert is named exactly 28 times by the tokens of every device.
All inputs are finite; a program needn't handle non-finite values.
Results may differ from a plain program's by a relative error of at most 0.0057.
Values may be sent and summed in bfloat16 or wider, within the bound.
No kernel may reach another device: no remote copies, remote signals or barrier semaphores. Data moves between devices by JAX's collectives and lax.ppermute only.
A program may use at most 128 MiB of HBM per device.

v0:
```python
import functools

import jax
import jax.numpy as jnp
from jax import lax
from jax.experimental import pallas as pl
from jax.experimental.pallas import tpu as pltpu
from jax.sharding import PartitionSpec as P

LANES = 128
IN_VMEM = pl.BlockSpec(memory_space=pltpu.VMEM)
IN_HBM = pl.BlockSpec(memory_space=pltpu.HBM)
DEPTH_STEP = 512
HIDDEN_STEP = 256
PASS_ROWS = 192
SCOPED_BYTES = 8 * 1024 * 1024
KEPT_BYTES = 32 * 1024 * 1024


def in_hbm(array):
    return pltpu.with_memory_space_constraint(array, pltpu.HBM)


def even_split(size, most):
    part = most
    while size % part:
        part //= 2
    return part


def chip_ring(chips):
    across = max(d for d in range(1, chips + 1) if chips % d == 0 and d * d <= chips)
    down = chips // across
    if across == 1 or down % 2:
        return list(range(chips))
    ring = []
    for row in range(down):
        columns = list(range(1, across))
        ring += [row * across + column for column in (columns if row % 2 == 0 else columns[::-1])]
    return [0] + ring + [row * across for row in range(down - 1, 0, -1)]


def ring_pairs(ring, way):
    count = len(ring)
    pairs = []
    for at, chip in enumerate(ring):
        for core in (0, 1):
            step = way if core == at % 2 else -way
            pairs.append((2 * chip + core, 2 * ring[(at + step) % count] + 1 - core))
    return pairs


def pack_kernel(tokens_ref, ids_ref, gates_ref, out_ref, ids_buf, gates_buf, sems):
    width = tokens_ref.shape[1]
    copies = [
        pltpu.make_async_copy(ids_ref, ids_buf, sems.at[0]),
        pltpu.make_async_copy(gates_ref, gates_buf, sems.at[1]),
        pltpu.make_async_copy(tokens_ref, out_ref.at[:, pl.ds(0, width)], sems.at[2]),
    ]
    for copy in copies:
        copy.start()
    for copy in copies[:2]:
        copy.wait()
    rest = gates_buf[...]
    parts = [ids_buf[...].astype(jnp.float32)]
    for _ in range(3):
        parts.append(rest.astype(jnp.bfloat16).astype(jnp.float32))
        rest = rest - parts[-1]
    stacked = jnp.concatenate(parts, axis=0)
    shape = (stacked.shape[0], out_ref.shape[1] - width)
    unit = lax.broadcasted_iota(jnp.int32, shape, 0) == lax.broadcasted_iota(jnp.int32, shape, 1)
    route = lax.dot_general(
        stacked.astype(jnp.bfloat16),
        unit.astype(jnp.float32).astype(jnp.bfloat16),
        (((0,), (0,)), ((), ())),
        preferred_element_type=jnp.float32,
    )
    out_ref[:, width:] = route.astype(jnp.bfloat16)
    copies[2].wait()


def pack_rows(tokens, expert_ids, gate_weights, made):
    rows, width = tokens.shape
    extra = -(-4 * expert_ids.shape[1] // LANES) * LANES
    ids, gates = expert_ids.T, gate_weights.T
    return pl.pallas_call(
        pack_kernel,
        out_shape=made((rows, width + extra), jnp.bfloat16),
        in_specs=[IN_HBM] * 3,
        out_specs=IN_VMEM,
        scratch_shapes=[
            pltpu.VMEM(ids.shape, ids.dtype),
            pltpu.VMEM(gates.shape, gates.dtype),
            pltpu.SemaphoreType.DMA((3,)),
        ],
        compiler_params=pltpu.CompilerParams(vmem_limit_bytes=SCOPED_BYTES),
    )(in_hbm(tokens), in_hbm(ids), in_hbm(gates))


def row_scale(route, expert, top_count):
    route = route.astype(jnp.float32)
    chosen = (route[:, :top_count] == expert.astype(jnp.float32)).astype(jnp.float32)
    weight = sum(route[:, top_count * part : top_count * (part + 1)] for part in (1, 2, 3))
    return jnp.sum(chosen * weight, axis=1, keepdims=True)


def expert_kernel(blocks, flips, with_prior, top_count, *refs):
    row_refs, refs = refs[:blocks], refs[blocks:]
    weight_refs, refs = refs[: 3 * len(flips)], refs[3 * len(flips) :]
    prior_refs, refs = (refs[:blocks], refs[blocks:]) if with_prior else ((), refs)
    out_refs, (rows_buf, total) = refs[:blocks], refs[blocks:]
    block_rows, width = out_refs[0].shape
    real = blocks * block_rows
    me = lax.axis_index("expert")
    for at in range(rows_buf.shape[0] // block_rows):
        rows_buf[pl.ds(at * block_rows, block_rows), :] = row_refs[at % blocks][...]
    for at in range(blocks if with_prior else 0):
        total[pl.ds(at * block_rows, block_rows), :] = prior_refs[at][...]
    rows = rows_buf[:, :width]
    for at, flip in enumerate(flips):
        gate_ref, up_ref, down_ref = weight_refs[3 * at : 3 * at + 3]
        scale = row_scale(rows_buf[:real, width:], me ^ flip, top_count)
        gate_part = jnp.dot(rows, gate_ref[0], preferred_element_type=jnp.float32)
        up_part = jnp.dot(rows, up_ref[0], preferred_element_type=jnp.float32)
        hidden = (gate_part / (1.0 + jnp.exp(-gate_part)) * up_part).astype(jnp.bfloat16)
        result = jnp.dot(hidden, down_ref[0], preferred_element_type=jnp.float32)[:real] * scale
        if at or with_prior:
            total[...] += result
        else:
            total[...] = result
    for at in range(blocks):
        out_refs[at][...] = total[pl.ds(at * block_rows, block_rows), :]


def run_experts(made, top_count, row_blocks, flips, weights, prior=()):
    blocks, experts = len(row_blocks), len(weights)
    block_rows, row_width = row_blocks[0].shape
    _, width, hidden_width = weights[0][0].shape
    total = blocks * block_rows
    padded = max(total, PASS_ROWS // block_rows * block_rows) if experts == 1 else total
    return pl.pallas_call(
        functools.partial(expert_kernel, blocks, flips, bool(prior), top_count),
        out_shape=[made((block_rows, width), jnp.float32)] * blocks,
        in_specs=[IN_VMEM] * (blocks + 3 * experts + len(prior)),
        out_specs=[IN_VMEM] * blocks,
        scratch_shapes=[
            pltpu.VMEM((padded, row_width), jnp.bfloat16),
            pltpu.VMEM((total, width), jnp.float32),
        ],
        compiler_params=pltpu.CompilerParams(vmem_limit_bytes=SCOPED_BYTES),
        cost_estimate=pl.CostEstimate(
            flops=6 * total * width * hidden_width * experts,
            bytes_accessed=2 * (3 * width * hidden_width * experts + 2 * total * width),
            transcendentals=total * hidden_width * experts,
        ),
    )(
        *(made.pin(block) for block in row_blocks),
        *(made.pin(array) for weight in weights for array in weight),
        *(made.pin(block) for block in prior),
    )


def first_kernel(rows_ref, gate_in, up_in, hidden_ref, gate_ref, up_ref, parts, sems):
    width = gate_ref.shape[1]
    deep = even_split(width, DEPTH_STEP)
    sides = ((gate_in, gate_ref), (up_in, up_ref))

    def copies(at):
        span = pl.ds(at * deep, deep)
        return [
            pltpu.make_async_copy(source.at[0, span, :], kept.at[0, span, :], sems.at[side, at])
            for side, (source, kept) in enumerate(sides)
        ]

    steps = width // deep
    for at in range(steps):
        for copy in copies(at):
            copy.start()
    for at in range(steps):
        for copy in copies(at):
            copy.wait()
        span = pl.ds(at * deep, deep)
        for side, (_, kept) in enumerate(sides):
            now = jnp.dot(rows_ref[:, span], kept[0, span, :], preferred_element_type=jnp.float32)
            if at == 0:
                parts[side] = now
            else:
                parts[side] += now
    gate_part, up_part = parts[0], parts[1]
    hidden_ref[...] = (gate_part / (1.0 + jnp.exp(-gate_part)) * up_part).astype(jnp.bfloat16)


def second_kernel(top_count, rows_ref, hidden_ref, down_in, out_ref, down_ref, sems):
    hidden_width, width = down_ref.shape[1:]
    wide = even_split(hidden_width, HIDDEN_STEP)

    def copy(at):
        span = pl.ds(at * wide, wide)
        return pltpu.make_async_copy(down_in.at[0, span, :], down_ref.at[0, span, :], sems.at[at])

    steps = hidden_width // wide
    for at in range(steps):
        copy(at).start()
    scale = row_scale(rows_ref[:, width:], lax.axis_index("expert"), top_count)
    for at in range(steps):
        copy(at).wait()
        span = pl.ds(at * wide, wide)
        now = jnp.dot(hidden_ref[:, span], down_ref[0, span, :], preferred_element_type=jnp.float32)
        if at == 0:
            out_ref[...] = now
        else:
            out_ref[...] += now
    out_ref[...] = out_ref[...] * scale


def take_inputs_in(made, block, gate, up):
    _, width, hidden_width = gate.shape
    rows = block.shape[0]
    hidden, gate, up = pl.pallas_call(
        first_kernel,
        out_shape=[made((rows, hidden_width), jnp.bfloat16)] + [made(gate.shape, gate.dtype)] * 2,
        in_specs=[IN_VMEM] + [IN_HBM] * 2,
        out_specs=[IN_VMEM] * 3,
        scratch_shapes=[
            pltpu.VMEM((2, rows, hidden_width), jnp.float32),
            pltpu.SemaphoreType.DMA((2, width // even_split(width, DEPTH_STEP))),
        ],
        compiler_params=pltpu.CompilerParams(vmem_limit_bytes=SCOPED_BYTES),
        cost_estimate=pl.CostEstimate(
            flops=4 * rows * width * hidden_width,
            bytes_accessed=4 * width * hidden_width,
            transcendentals=rows * hidden_width,
        ),
    )(made.pin(block), in_hbm(gate), in_hbm(up))
    return hidden, gate, up


def take_output_in(made, top_count, block, hidden, down):
    _, hidden_width, width = down.shape
    rows = block.shape[0]
    return pl.pallas_call(
        functools.partial(second_kernel, top_count),
        out_shape=[made((rows, width), jnp.float32), made(down.shape, down.dtype)],
        in_specs=[IN_VMEM] * 2 + [IN_HBM],
        out_specs=[IN_VMEM] * 2,
        scratch_shapes=[
            pltpu.SemaphoreType.DMA((hidden_width // even_split(hidden_width, HIDDEN_STEP),))
        ],
        compiler_params=pltpu.CompilerParams(vmem_limit_bytes=SCOPED_BYTES),
        cost_estimate=pl.CostEstimate(
            flops=2 * rows * width * hidden_width,
            bytes_accessed=2 * width * hidden_width,
            transcendentals=0,
        ),
    )(made.pin(block), made.pin(hidden), in_hbm(down))


class InVmem:
    def __call__(self, shape, dtype):
        return pltpu.VMEM(shape, dtype)

    def pin(self, array):
        return pltpu.with_memory_space_constraint(array, pltpu.VMEM)


class Anywhere:
    def __call__(self, shape, dtype):
        return jax.ShapeDtypeStruct(shape, dtype)

    def pin(self, array):
        return array


def add_rounded(*terms):
    return sum(term.astype(jnp.float32) for term in terms).astype(jnp.bfloat16)


def shards(tokens, expert_ids, gate_weights, w_gate, w_up, w_down):
    local, width = tokens.shape
    top_count = expert_ids.shape[1]
    devices = lax.axis_size("expert")
    ring = chip_ring(devices // 2)
    ways = (ring_pairs(ring, 1), ring_pairs(ring, -1))
    siblings = [(at, at ^ 1) for at in range(devices)]
    hops = (len(ring) // 2, (len(ring) - 1) // 2)
    own = (w_gate, w_up, w_down)
    weight_bytes = 2 * sum(array.size * array.dtype.itemsize for array in own)
    kept_bytes = weight_bytes + len(ring) * local * width * 6
    made = InVmem() if kept_bytes <= KEPT_BYTES else Anywhere()
    run = functools.partial(run_experts, made, top_count)
    after = lax.optimization_barrier

    def outward(block, way):
        return lax.ppermute(block, "expert", ways[way])

    def homeward(block, way):
        return lax.ppermute(block, "expert", ways[1 - way])

    first = pack_rows(tokens, expert_ids, gate_weights, made)
    other = tuple(lax.ppermute(array, "expert", siblings) for array in own)

    rows = {(0, 0): first}
    partial = {}
    if hops[0]:
        rows[0, 1] = outward(first, 0)
    hidden, gate, up = take_inputs_in(made, first, w_gate, w_up)
    if hops[1]:
        later, hidden = after((first, hidden))
        rows[1, 1] = outward(later, 1)
    partial[0, 0], down = take_output_in(made, top_count, first, hidden, w_down)
    own = (gate, up, down)
    if hops[0]:
        rows[0, 1], partial[0, 0] = after((rows[0, 1], partial[0, 0]))
    for hop in range(2, hops[0] + 1):
        rows[0, hop] = outward(rows[0, hop - 1], 0)
        keys = [(0, hop - 1)] + [(1, hop - 2)] * (hop > 2)
        results = run([rows[key] for key in keys], (0,), [own])
        rows[1, hop - 1], results = after((rows[1, hop - 1], results))
        partial.update(zip(keys, results))
        if hop <= hops[1]:
            rows[1, hop] = outward(rows[1, hop - 1], 1)
    keys = [key for key in rows if key not in partial]
    if keys:
        results = run([rows[key] for key in keys], (0, 1), [own, other])
        partial.update(zip(keys, results))

    def sibling_sums(keys, prior):
        return run([rows[key] for key in keys], (1,), [other], prior)

    if hops[0] < 2:
        partial[0, 0] = sibling_sums([(0, 0)], [partial[0, 0]])[0]
    arrived = [None, None]
    level = list(hops)
    while level[0]:
        values = [None, None]
        values[0] = add_rounded(partial[0, level[0]], *[x for x in arrived[:1] if x is not None])
        arrived[0] = homeward(values[0], 0)
        keys = [(way, at - 1) for way, at in enumerate(level) if at > 1]
        keys = [key for key in keys if key in partial and key != (1, hops[0] - 1)]
        keys += [(0, 0)] * (level[0] == 2)
        waiting = arrived[1] if arrived[1] is not None else partial.get((1, level[1]))
        if keys:
            prior, _ = after(([partial[key] for key in keys], values[0]))
            waiting, results = after((waiting, sibling_sums(keys, prior)))
            partial.update(zip(keys, results))
        if level[1]:
            values[1] = add_rounded(*([waiting] if arrived[1] is None else [waiting, partial[1, level[1]]]))
            arrived[1] = homeward(values[1], 1)
        elif arrived[1] is not None:
            arrived[1] = waiting
        level = [max(at - 1, 0) for at in level]
    total = partial[0, 0]
    if arrived[1] is not None:
        total, arrived[0] = after((total + arrived[1].astype(jnp.float32), arrived[0]))
    return add_rounded(total, *[value for value in arrived[:1] if value is not None])


def solution(mesh):
    placed = (
        P(("groups", "expert"), None),
        P(("groups", "expert"), None),
        P(("groups", "expert"), None),
        P("expert", None, None),
        P("expert", None, None),
        P("expert", None, None),
    )
    return jax.shard_map(
        shards, mesh=mesh, in_specs=placed, out_specs=P(("groups", "expert"), None), check_vma=False
    )
```

profile of v0, /device:TPU:0, one launch (start us, length us, event | category | flops | bytes accessed | tf_op | source)
XLA Modules:
  0.0 62.0 jit_solution(5180042480835559043)
XLA Ops:
  0.0 0.5 collective-permute-start.7
  0.5 0.1 collective-permute-start.8
  0.5 0.5 collective-permute-start.9
  1.0 1.0 %shard_map.64.rows_ref.refs_1_ = bf16[64,2176]{1,0:T(8,128)(2,1)S(1)} custom-call(bf16[64,2048]{1,0:T(8,128)(2,1)} %tokens_ref.1, s32[8,64]{1,0:T(8,128)} %bitcast.2, f32[8,64]{1,0:T(8,128)} %bitcast.3), custom_call_target="tpu_custom_call" | custom-call | tf_op jit(solution)/shard_map/pallas_call | solution.py:86
  2.0 2.7 %collective-permute-start.1 = (bf16[64,2176]{1,0:T(8,128)(2,1)S(1)}, bf16[64,2176]{1,0:T(8,128)(2,1)S(1)}, u32[]{:S(2)}, u32[]{:S(2)}) collective-permute-start(bf16[64,2176]{1,0:T(8,128)(2,1)S(1)} %shard_map.64.rows_ref.refs_1_), channel_id=1, source_target_pairs={{0,3},{1,4},{2,1},{3,6},{6,11},{7,2},{10,7},{11,14},{14,13},{15,10... | collective-permute-start | bytes 835592 | tf_op jit(solution)/shard_map/ppermute | solution.py:294
  4.7 3.2 %shard_map.65 = (bf16[64,768]{1,0:T(8,128)(2,1)S(1)}, bf16[1,2048,768]{2,1,0:T(8,128)(2,1)S(1)}, bf16[1,2048,768]{2,1,0:T(8,128)(2,1)S(1)}) custom-call(bf16[64,2176]{1,0:T(8,128)(2,1)S(1)} %shard_map.64.rows_ref.refs_1_, bf16[1,2048,768]{2,1,0:T(8,128)(2,1)} %gate_in.1, bf16[1,2048,768]{2,1,0:T(8,128)(2,1)} %up_in.1), custom_call_target="tpu_custom_call" | custom-call | flops 402653184 | bytes 6291456 | tf_op jit(solution)/shard_map/pallas_call | solution.py:219
  7.9 0.1 collective-permute-start
  8.0 2.2 %shard_map.66 = (f32[64,2048]{1,0:T(8,128)S(1)}, bf16[1,768,2048]{2,1,0:T(8,128)(2,1)S(1)}) custom-call(bf16[64,2176]{1,0:T(8,128)(2,1)S(1)} %shard_map.64.rows_ref.refs_1_, bf16[64,768]{1,0:T(8,128)(2,1)S(1)} %get-tuple-element.53.hidden_ref, bf16[1,768,2048]{2,1,0:T(8,128)(2,1)} %down_in.1), custom_call_target="tpu_custom_call" | custom-call | flops 201326592 | bytes 3145728 | tf_op jit(solution)/shard_map/pallas_call | solution.py:241
  10.2 0.0 collective-permute-done.1.refs_0_
  10.2 1.7 %collective-permute-start.3 = (bf16[64,2176]{1,0:T(8,128)(2,1)S(1)}, bf16[64,2176]{1,0:T(8,128)(2,1)S(1)}, u32[]{:S(2)}, u32[]{:S(2)}) collective-permute-start(bf16[64,2176]{1,0:T(8,128)(2,1)S(1)} %collective-permute-done.1.refs_0_), channel_id=1, source_target_pairs={{0,3},{1,4},{2,1},{3,6},{6,11},{7,2},{10,7},{11,14},{14,13},{15,10... | collective-permute-start | bytes 835592 | tf_op jit(solution)/shard_map/ppermute | solution.py:294
  12.0 2.0 %shard_map.67.refs_5_ = f32[64,2048]{1,0:T(8,128)S(1)} custom-call(bf16[64,2176]{1,0:T(8,128)(2,1)S(1)} %collective-permute-done.1.refs_0_, bf16[1,2048,768]{2,1,0:T(8,128)(2,1)S(1)} %get-tuple-element.56.refs_1_.refs_2_, bf16[1,2048,768]{2,1,0:T(8,128)(2,1)S(1)} %get-tuple-element.57.refs_2_.refs_3_, bf16[1,768,2048]{2,1,0:T(8,128)(2,1)S(1)} %get-tuple-element.58.refs_3_.refs_4_), custom_call_target="tpu_custom_call" | custom-call | flops 603979776 | bytes 9961472 | tf_op jit(solution)/shard_map/pallas_call | solution.py:141
  14.0 0.3 collective-permute-done.refs_1_
  14.3 0.0 collective-permute-start.2
  14.4 2.8 %collective-permute-done.3.refs_0_ = bf16[64,2176]{1,0:T(8,128)(2,1)S(1)} collective-permute-done((bf16[64,2176]{1,0:T(8,128)(2,1)S(1)}, bf16[64,2176]{1,0:T(8,128)(2,1)S(1)}, u32[]{:S(2)}, u32[]{:S(2)}) %collective-permute-start.3) | collective-permute-done | bytes 278560 | tf_op jit(solution)/shard_map/ppermute | solution.py:294
  17.2 1.5 %collective-permute-start.5 = (bf16[64,2176]{1,0:T(8,128)(2,1)S(1)}, bf16[64,2176]{1,0:T(8,128)(2,1)S(1)}, u32[]{:S(2)}, u32[]{:S(2)}) collective-permute-start(bf16[64,2176]{1,0:T(8,128)(2,1)S(1)} %collective-permute-done.3.refs_0_), channel_id=1, source_target_pairs={{0,3},{1,4},{2,1},{3,6},{6,11},{7,2},{10,7},{11,14},{14,13},{15,10... | collective-permute-start | bytes 835592 | tf_op jit(solution)/shard_map/ppermute | solution.py:294
  18.7 2.1 %shard_map.68 = (f32[64,2048]{1,0:T(8,128)S(1)}, f32[64,2048]{1,0:T(8,128)S(1)}) custom-call(bf16[64,2176]{1,0:T(8,128)(2,1)S(1)} %collective-permute-done.3.refs_0_, bf16[64,2176]{1,0:T(8,128)(2,1)S(1)} %collective-permute-done.refs_1_, bf16[1,2048,768]{2,1,0:T(8,128)(2,1)S(1)} %get-tuple-element.56.refs_1_.refs_2_, ...), custom_call_target="tpu_custom_call" | custom-call | flops 1207959552 | bytes 10485760 | tf_op jit(solution)/shard_map/pallas_call | solution.py:141
  20.8 0.0 collective-permute-done.2.refs_1_
  20.8 0.3 collective-permute-start.4
  21.0 3.2 %collective-permute-done.5.refs_0_ = bf16[64,2176]{1,0:T(8,128)(2,1)S(1)} collective-permute-done((bf16[64,2176]{1,0:T(8,128)(2,1)S(1)}, bf16[64,2176]{1,0:T(8,128)(2,1)S(1)}, u32[]{:S(2)}, u32[]{:S(2)}) %collective-permute-start.5) | collective-permute-done | bytes 278560 | tf_op jit(solution)/shard_map/ppermute | solution.py:294
  24.3 0.7 %collective-permute-start.6 = (bf16[64,2176]{1,0:T(8,128)(2,1)S(1)}, bf16[64,2176]{1,0:T(8,128)(2,1)S(1)}, u32[]{:S(2)}, u32[]{:S(2)}) collective-permute-start(bf16[64,2176]{1,0:T(8,128)(2,1)S(1)} %collective-permute-done.5.refs_0_), channel_id=1, source_target_pairs={{0,3},{1,4},{2,1},{3,6},{6,11},{7,2},{10,7},{11,14},{14,13},{15,10... | collective-permute-start | bytes 835592 | tf_op jit(solution)/shard_map/ppermute | solution.py:294
  25.0 2.0 %shard_map.69 = (f32[64,2048]{1,0:T(8,128)S(1)}, f32[64,2048]{1,0:T(8,128)S(1)}) custom-call(bf16[64,2176]{1,0:T(8,128)(2,1)S(1)} %collective-permute-done.5.refs_0_, bf16[64,2176]{1,0:T(8,128)(2,1)S(1)} %collective-permute-done.2.refs_1_, bf16[1,2048,768]{2,1,0:T(8,128)(2,1)S(1)} %get-tuple-element.56.refs_1_.refs_2_, ...), custom_call_target="tpu_custom_call" | custom-call | flops 1207959552 | bytes 10485760 | tf_op jit(solution)/shard_map/pallas_call | solution.py:141
  27.0 1.1 %collective-permute-done.4.refs_0_ = bf16[64,2176]{1,0:T(8,128)(2,1)S(1)} collective-permute-done((bf16[64,2176]{1,0:T(8,128)(2,1)S(1)}, bf16[64,2176]{1,0:T(8,128)(2,1)S(1)}, u32[]{:S(2)}, u32[]{:S(2)}) %collective-permute-start.4) | collective-permute-done | bytes 278560 | tf_op jit(solution)/shard_map/ppermute | solution.py:294
  28.1 3.5 %collective-permute-done.6.refs_1_ = bf16[64,2176]{1,0:T(8,128)(2,1)S(1)} collective-permute-done((bf16[64,2176]{1,0:T(8,128)(2,1)S(1)}, bf16[64,2176]{1,0:T(8,128)(2,1)S(1)}, u32[]{:S(2)}, u32[]{:S(2)}) %collective-permute-start.6) | collective-permute-done | bytes 278560 | tf_op jit(solution)/shard_map/ppermute | solution.py:294
  31.6 0.0 collective-permute-done.7.refs_5_.refs_2_
  31.6 0.0 collective-permute-done.8.refs_6_.refs_3_
  31.6 0.0 collective-permute-done.9.refs_7_.refs_4_
  31.6 2.8 %shard_map.70 = (f32[64,2048]{1,0:T(8,128)S(1)}, f32[64,2048]{1,0:T(8,128)S(1)}) custom-call(bf16[64,2176]{1,0:T(8,128)(2,1)S(1)} %collective-permute-done.4.refs_0_, bf16[64,2176]{1,0:T(8,128)(2,1)S(1)} %collective-permute-done.6.refs_1_, bf16[1,2048,768]{2,1,0:T(8,128)(2,1)S(1)} %get-tuple-element.56.refs_1_.refs_2_, ...), custom_call_target="tpu_custom_call" | custom-call | flops 2415919104 | bytes 19922944 | tf_op jit(solution)/shard_map/pallas_call | solution.py:141
  34.4 0.4 collective-permute-start.11
  34.8 2.1 %shard_map.71 = (f32[64,2048]{1,0:T(8,128)S(1)}, f32[64,2048]{1,0:T(8,128)S(1)}) custom-call(bf16[64,2176]{1,0:T(8,128)(2,1)S(1)} %collective-permute-done.5.refs_0_, bf16[64,2176]{1,0:T(8,128)(2,1)S(1)} %collective-permute-done.2.refs_1_, bf16[1,2048,768]{2,1,0:T(8,128)(2,1)S(1)} %collective-permute-done.7.refs_5_.refs_2_, ...), custom_call_target="tpu_custom_call" | custom-call | flops 1207959552 | bytes 10485760 | tf_op jit(solution)/shard_map/pallas_call | solution.py:141
  37.0 1.6 %collective-permute-start.10 = (bf16[64,2048]{1,0:T(8,128)(2,1)S(1)}, bf16[64,2048]{1,0:T(8,128)(2,1)S(1)}, u32[]{:S(2)}, u32[]{:S(2)}) collective-permute-start(bf16[64,2048]{1,0:T(8,128)(2,1)S(1)} %convert_element_type.46), channel_id=1, source_target_pairs={{0,3},{1,4},{2,1},{3,6},{6,11},{7,2},{10,7},{11,14},{14,13},{15,10... | collective-permute-start | bytes 786440 | tf_op jit(solution)/shard_map/ppermute | solution.py:297
  38.6 1.9 %collective-permute-done.11 = bf16[64,2048]{1,0:T(8,128)(2,1)S(1)} collective-permute-done((bf16[64,2048]{1,0:T(8,128)(2,1)S(1)}, bf16[64,2048]{1,0:T(8,128)(2,1)S(1)}, u32[]{:S(2)}, u32[]{:S(2)}) %collective-permute-start.11) | collective-permute-done | bytes 262176 | tf_op jit(solution)/shard_map/ppermute | solution.py:297
  40.5 0.6 %collective-permute-start.13 = (bf16[64,2048]{1,0:T(8,128)(2,1)S(1)}, bf16[64,2048]{1,0:T(8,128)(2,1)S(1)}, u32[]{:S(2)}, u32[]{:S(2)}) collective-permute-start(bf16[64,2048]{1,0:T(8,128)(2,1)S(1)} %add_convert_fusion.5), channel_id=1, source_target_pairs={{0,5},{1,2},{2,7},{3,0},{6,3},{7,10},{10,15},{11,6},{14,11},{15,12... | collective-permute-start | bytes 786440 | tf_op jit(solution)/shard_map/ppermute | solution.py:297
  41.1 2.1 %shard_map.72 = (f32[64,2048]{1,0:T(8,128)S(1)}, f32[64,2048]{1,0:T(8,128)S(1)}) custom-call(bf16[64,2176]{1,0:T(8,128)(2,1)S(1)} %collective-permute-done.3.refs_0_, bf16[64,2176]{1,0:T(8,128)(2,1)S(1)} %collective-permute-done.refs_1_, bf16[1,2048,768]{2,1,0:T(8,128)(2,1)S(1)} %collective-permute-done.7.refs_5_.refs_2_, ...), custom_call_target="tpu_custom_call" | custom-call | flops 1207959552 | bytes 10485760 | tf_op jit(solution)/shard_map/pallas_call | solution.py:141
  43.2 0.8 %collective-permute-done.10 = bf16[64,2048]{1,0:T(8,128)(2,1)S(1)} collective-permute-done((bf16[64,2048]{1,0:T(8,128)(2,1)S(1)}, bf16[64,2048]{1,0:T(8,128)(2,1)S(1)}, u32[]{:S(2)}, u32[]{:S(2)}) %collective-permute-start.10) | collective-permute-done | bytes 262176 | tf_op jit(solution)/shard_map/ppermute | solution.py:297
  44.0 0.1 add_convert_fusion.4
  44.1 0.7 %collective-permute-start.12 = (bf16[64,2048]{1,0:T(8,128)(2,1)S(1)}, bf16[64,2048]{1,0:T(8,128)(2,1)S(1)}, u32[]{:S(2)}, u32[]{:S(2)}) collective-permute-start(bf16[64,2048]{1,0:T(8,128)(2,1)S(1)} %add_convert_fusion.4), channel_id=1, source_target_pairs={{0,3},{1,4},{2,1},{3,6},{6,11},{7,2},{10,7},{11,14},{14,13},{15,10... | collective-permute-start | bytes 786440 | tf_op jit(solution)/shard_map/ppermute | solution.py:297
  44.8 2.4 %collective-permute-done.13 = bf16[64,2048]{1,0:T(8,128)(2,1)S(1)} collective-permute-done((bf16[64,2048]{1,0:T(8,128)(2,1)S(1)}, bf16[64,2048]{1,0:T(8,128)(2,1)S(1)}, u32[]{:S(2)}, u32[]{:S(2)}) %collective-permute-start.13) | collective-permute-done | bytes 262176 | tf_op jit(solution)/shard_map/ppermute | solution.py:297
  47.2 0.1 add_convert_fusion.3
  47.2 0.1 collective-permute-start.15
  47.4 2.1 %shard_map.73 = (f32[64,2048]{1,0:T(8,128)S(1)}, f32[64,2048]{1,0:T(8,128)S(1)}) custom-call(bf16[64,2176]{1,0:T(8,128)(2,1)S(1)} %collective-permute-done.1.refs_0_, bf16[64,2176]{1,0:T(8,128)(2,1)S(1)} %shard_map.64.rows_ref.refs_1_, bf16[1,2048,768]{2,1,0:T(8,128)(2,1)S(1)} %collective-permute-done.7.refs_5_.refs_2_, ...), custom_call_target="tpu_custom_call" | custom-call | flops 1207959552 | bytes 10485760 | tf_op jit(solution)/shard_map/pallas_call | solution.py:141
  49.4 0.6 %collective-permute-done.12 = bf16[64,2048]{1,0:T(8,128)(2,1)S(1)} collective-permute-done((bf16[64,2048]{1,0:T(8,128)(2,1)S(1)}, bf16[64,2048]{1,0:T(8,128)(2,1)S(1)}, u32[]{:S(2)}, u32[]{:S(2)}) %collective-permute-start.12) | collective-permute-done | bytes 262176 | tf_op jit(solution)/shard_map/ppermute | solution.py:297
  50.0 0.1 add_convert_fusion.2
  50.1 1.1 %collective-permute-start.14 = (bf16[64,2048]{1,0:T(8,128)(2,1)S(1)}, bf16[64,2048]{1,0:T(8,128)(2,1)S(1)}, u32[]{:S(2)}, u32[]{:S(2)}) collective-permute-start(bf16[64,2048]{1,0:T(8,128)(2,1)S(1)} %add_convert_fusion.2), channel_id=1, source_target_pairs={{0,3},{1,4},{2,1},{3,6},{6,11},{7,2},{10,7},{11,14},{14,13},{15,10... | collective-permute-start | bytes 786440 | tf_op jit(solution)/shard_map/ppermute | solution.py:297
  51.2 2.9 %collective-permute-done.15 = bf16[64,2048]{1,0:T(8,128)(2,1)S(1)} collective-permute-done((bf16[64,2048]{1,0:T(8,128)(2,1)S(1)}, bf16[64,2048]{1,0:T(8,128)(2,1)S(1)}, u32[]{:S(2)}, u32[]{:S(2)}) %collective-permute-start.15) | collective-permute-done | bytes 262176 | tf_op jit(solution)/shard_map/ppermute | solution.py:297
  54.2 0.1 collective-permute-start.16
  54.2 1.9 %collective-permute-done.14 = bf16[64,2048]{1,0:T(8,128)(2,1)S(1)} collective-permute-done((bf16[64,2048]{1,0:T(8,128)(2,1)S(1)}, bf16[64,2048]{1,0:T(8,128)(2,1)S(1)}, u32[]{:S(2)}, u32[]{:S(2)}) %collective-permute-start.14) | collective-permute-done | bytes 262176 | tf_op jit(solution)/shard_map/ppermute | solution.py:297
  56.1 0.1 convert_add_fusion
  56.1 5.1 %collective-permute-done.16 = bf16[64,2048]{1,0:T(8,128)(2,1)S(1)} collective-permute-done((bf16[64,2048]{1,0:T(8,128)(2,1)S(1)}, bf16[64,2048]{1,0:T(8,128)(2,1)S(1)}, u32[]{:S(2)}, u32[]{:S(2)}) %collective-permute-start.16) | collective-permute-done | bytes 262176 | tf_op jit(solution)/shard_map/ppermute | solution.py:297
  61.3 0.8 %add_convert_fusion = bf16[64,2048]{1,0:T(8,128)(2,1)} fusion(f32[64,2048]{1,0:T(8,128)S(1)} %convert_add_fusion, bf16[64,2048]{1,0:T(8,128)(2,1)S(1)} %collective-permute-done.16), kind=kLoop, calls=%fused_computation | loop fusion | flops 393216 | bytes 1048576 | tf_op jit(solution)/shard_map/convert_element_type | solution.py:275
  (4 shorter events, 0.2 us)
Async XLA Ops:
  0.0 31.6 %collective-permute-start.7 = (bf16[1,2048,768]{2,1,0:T(8,128)(2,1)}, bf16[1,2048,768]{2,1,0:T(8,128)(2,1)S(1)}, u32[]{:S(2)}, u32[]{:S(2)}) collective-permute-start(bf16[1,2048,768]{2,1,0:T(8,128)(2,1)} %gate_in.1), channel_id=1, source_target_pairs={{0,1},{1,0},{2,3},{3,2},{4,5},{5,4},{6,7},{7,6},{8,9},{9,8},{10,11... | collective-permute-start | bytes 9437192 | tf_op jit(solution)/shard_map/ppermute | solution.py:300
  0.5 31.1 %collective-permute-start.8 = (bf16[1,2048,768]{2,1,0:T(8,128)(2,1)}, bf16[1,2048,768]{2,1,0:T(8,128)(2,1)S(1)}, u32[]{:S(2)}, u32[]{:S(2)}) collective-permute-start(bf16[1,2048,768]{2,1,0:T(8,128)(2,1)} %up_in.1), channel_id=1, source_target_pairs={{0,1},{1,0},{2,3},{3,2},{4,5},{5,4},{6,7},{7,6},{8,9},{9,8},{10,11... | collective-permute-start | bytes 9437192 | tf_op jit(solution)/shard_map/ppermute | solution.py:300
  0.5 31.1 %collective-permute-start.9 = (bf16[1,768,2048]{2,1,0:T(8,128)(2,1)}, bf16[1,768,2048]{2,1,0:T(8,128)(2,1)S(1)}, u32[]{:S(2)}, u32[]{:S(2)}) collective-permute-start(bf16[1,768,2048]{2,1,0:T(8,128)(2,1)} %down_in.1), channel_id=1, source_target_pairs={{0,1},{1,0},{2,3},{3,2},{4,5},{5,4},{6,7},{7,6},{8,9},{9,8},{10,11... | collective-permute-start | bytes 9437192 | tf_op jit(solution)/shard_map/ppermute | solution.py:300
  2.0 8.3 %collective-permute-start.1 = (bf16[64,2176]{1,0:T(8,128)(2,1)S(1)}, bf16[64,2176]{1,0:T(8,128)(2,1)S(1)}, u32[]{:S(2)}, u32[]{:S(2)}) collective-permute-start(bf16[64,2176]{1,0:T(8,128)(2,1)S(1)} %shard_map.64.rows_ref.refs_1_), channel_id=1, source_target_pairs={{0,3},{1,4},{2,1},{3,6},{6,11},{7,2},{10,7},{11,14},{14,13},{15,10... | collective-permute-start | bytes 835592 | tf_op jit(solution)/shard_map/ppermute | solution.py:294
  7.9 6.4 %collective-permute-start = (bf16[64,2176]{1,0:T(8,128)(2,1)S(1)}, bf16[64,2176]{1,0:T(8,128)(2,1)S(1)}, u32[]{:S(2)}, u32[]{:S(2)}) collective-permute-start(bf16[64,2176]{1,0:T(8,128)(2,1)S(1)} %shard_map.64.rows_ref.refs_1_), channel_id=1, source_target_pairs={{0,5},{1,2},{2,7},{3,0},{6,3},{7,10},{10,15},{11,6},{14,11},{15,12... | collective-permute-start | bytes 835592 | tf_op jit(solution)/shard_map/ppermute | solution.py:294
  10.2 6.9 %collective-permute-start.3 = (bf16[64,2176]{1,0:T(8,128)(2,1)S(1)}, bf16[64,2176]{1,0:T(8,128)(2,1)S(1)}, u32[]{:S(2)}, u32[]{:S(2)}) collective-permute-start(bf16[64,2176]{1,0:T(8,128)(2,1)S(1)} %collective-permute-done.1.refs_0_), channel_id=1, source_target_pairs={{0,3},{1,4},{2,1},{3,6},{6,11},{7,2},{10,7},{11,14},{14,13},{15,10... | collective-permute-start | bytes 835592 | tf_op jit(solution)/shard_map/ppermute | solution.py:294
  14.3 6.4 %collective-permute-start.2 = (bf16[64,2176]{1,0:T(8,128)(2,1)S(1)}, bf16[64,2176]{1,0:T(8,128)(2,1)S(1)}, u32[]{:S(2)}, u32[]{:S(2)}) collective-permute-start(bf16[64,2176]{1,0:T(8,128)(2,1)S(1)} %collective-permute-done.refs_1_), channel_id=1, source_target_pairs={{0,5},{1,2},{2,7},{3,0},{6,3},{7,10},{10,15},{11,6},{14,11},{15,12... | collective-permute-start | bytes 835592 | tf_op jit(solution)/shard_map/ppermute | solution.py:294
  17.2 7.1 %collective-permute-start.5 = (bf16[64,2176]{1,0:T(8,128)(2,1)S(1)}, bf16[64,2176]{1,0:T(8,128)(2,1)S(1)}, u32[]{:S(2)}, u32[]{:S(2)}) collective-permute-start(bf16[64,2176]{1,0:T(8,128)(2,1)S(1)} %collective-permute-done.3.refs_0_), channel_id=1, source_target_pairs={{0,3},{1,4},{2,1},{3,6},{6,11},{7,2},{10,7},{11,14},{14,13},{15,10... | collective-permute-start | bytes 835592 | tf_op jit(solution)/shard_map/ppermute | solution.py:294
  20.8 7.3 %collective-permute-start.4 = (bf16[64,2176]{1,0:T(8,128)(2,1)S(1)}, bf16[64,2176]{1,0:T(8,128)(2,1)S(1)}, u32[]{:S(2)}, u32[]{:S(2)}) collective-permute-start(bf16[64,2176]{1,0:T(8,128)(2,1)S(1)} %collective-permute-done.2.refs_1_), channel_id=1, source_target_pairs={{0,5},{1,2},{2,7},{3,0},{6,3},{7,10},{10,15},{11,6},{14,11},{15,12... | collective-permute-start | bytes 835592 | tf_op jit(solution)/shard_map/ppermute | solution.py:294
  24.3 7.3 %collective-permute-start.6 = (bf16[64,2176]{1,0:T(8,128)(2,1)S(1)}, bf16[64,2176]{1,0:T(8,128)(2,1)S(1)}, u32[]{:S(2)}, u32[]{:S(2)}) collective-permute-start(bf16[64,2176]{1,0:T(8,128)(2,1)S(1)} %collective-permute-done.5.refs_0_), channel_id=1, source_target_pairs={{0,3},{1,4},{2,1},{3,6},{6,11},{7,2},{10,7},{11,14},{14,13},{15,10... | collective-permute-start | bytes 835592 | tf_op jit(solution)/shard_map/ppermute | solution.py:294
  34.4 6.0 %collective-permute-start.11 = (bf16[64,2048]{1,0:T(8,128)(2,1)S(1)}, bf16[64,2048]{1,0:T(8,128)(2,1)S(1)}, u32[]{:S(2)}, u32[]{:S(2)}) collective-permute-start(bf16[64,2048]{1,0:T(8,128)(2,1)S(1)} %convert_element_type.45), channel_id=1, source_target_pairs={{0,5},{1,2},{2,7},{3,0},{6,3},{7,10},{10,15},{11,6},{14,11},{15,12... | collective-permute-start | bytes 786440 | tf_op jit(solution)/shard_map/ppermute | solution.py:297
  37.0 7.1 %collective-permute-start.10 = (bf16[64,2048]{1,0:T(8,128)(2,1)S(1)}, bf16[64,2048]{1,0:T(8,128)(2,1)S(1)}, u32[]{:S(2)}, u32[]{:S(2)}) collective-permute-start(bf16[64,2048]{1,0:T(8,128)(2,1)S(1)} %convert_element_type.46), channel_id=1, source_target_pairs={{0,3},{1,4},{2,1},{3,6},{6,11},{7,2},{10,7},{11,14},{14,13},{15,10... | collective-permute-start | bytes 786440 | tf_op jit(solution)/shard_map/ppermute | solution.py:297
  40.5 6.7 %collective-permute-start.13 = (bf16[64,2048]{1,0:T(8,128)(2,1)S(1)}, bf16[64,2048]{1,0:T(8,128)(2,1)S(1)}, u32[]{:S(2)}, u32[]{:S(2)}) collective-permute-start(bf16[64,2048]{1,0:T(8,128)(2,1)S(1)} %add_convert_fusion.5), channel_id=1, source_target_pairs={{0,5},{1,2},{2,7},{3,0},{6,3},{7,10},{10,15},{11,6},{14,11},{15,12... | collective-permute-start | bytes 786440 | tf_op jit(solution)/shard_map/ppermute | solution.py:297
  44.1 6.0 %collective-permute-start.12 = (bf16[64,2048]{1,0:T(8,128)(2,1)S(1)}, bf16[64,2048]{1,0:T(8,128)(2,1)S(1)}, u32[]{:S(2)}, u32[]{:S(2)}) collective-permute-start(bf16[64,2048]{1,0:T(8,128)(2,1)S(1)} %add_convert_fusion.4), channel_id=1, source_target_pairs={{0,3},{1,4},{2,1},{3,6},{6,11},{7,2},{10,7},{11,14},{14,13},{15,10... | collective-permute-start | bytes 786440 | tf_op jit(solution)/shard_map/ppermute | solution.py:297
  47.2 6.9 %collective-permute-start.15 = (bf16[64,2048]{1,0:T(8,128)(2,1)S(1)}, bf16[64,2048]{1,0:T(8,128)(2,1)S(1)}, u32[]{:S(2)}, u32[]{:S(2)}) collective-permute-start(bf16[64,2048]{1,0:T(8,128)(2,1)S(1)} %add_convert_fusion.3), channel_id=1, source_target_pairs={{0,5},{1,2},{2,7},{3,0},{6,3},{7,10},{10,15},{11,6},{14,11},{15,12... | collective-permute-start | bytes 786440 | tf_op jit(solution)/shard_map/ppermute | solution.py:297
  50.1 6.0 %collective-permute-start.14 = (bf16[64,2048]{1,0:T(8,128)(2,1)S(1)}, bf16[64,2048]{1,0:T(8,128)(2,1)S(1)}, u32[]{:S(2)}, u32[]{:S(2)}) collective-permute-start(bf16[64,2048]{1,0:T(8,128)(2,1)S(1)} %add_convert_fusion.2), channel_id=1, source_target_pairs={{0,3},{1,4},{2,1},{3,6},{6,11},{7,2},{10,7},{11,14},{14,13},{15,10... | collective-permute-start | bytes 786440 | tf_op jit(solution)/shard_map/ppermute | solution.py:297
  54.2 7.1 %collective-permute-start.16 = (bf16[64,2048]{1,0:T(8,128)(2,1)S(1)}, bf16[64,2048]{1,0:T(8,128)(2,1)S(1)}, u32[]{:S(2)}, u32[]{:S(2)}) collective-permute-start(bf16[64,2048]{1,0:T(8,128)(2,1)S(1)} %add_convert_fusion.1), channel_id=1, source_target_pairs={{0,5},{1,2},{2,7},{3,0},{6,3},{7,10},{10,15},{11,6},{14,11},{15,12... | collective-permute-start | bytes 786440 | tf_op jit(solution)/shard_map/ppermute | solution.py:297
where the time goes:
time: 62.2 us; the launch traced here: 62 us
  waiting for transfers between devices  26.5 us (43%)
  Pallas kernels  21.6 us (35%)
  starting transfers between devices  12.6 us (20%)
  other arithmetic  1.15 us (2%)
    ppermute x7, waiting for transfers between devices, homeward(): return lax.ppermute(block, 'expert', ways[1 - way])  15.6 us
    pallas_call x7, Pallas kernels, run_experts(): pl.pallas_call(functools.partial(expert_kernel, blocks, flips, bool(prior...  15.1 us
    ppermute x7, waiting for transfers between devices, outward(): return lax.ppermute(block, 'expert', ways[way])  10.9 us
    ppermute x7, starting transfers between devices, outward(): return lax.ppermute(block, 'expert', ways[way])  7.04 us
    ppermute x7, starting transfers between devices, homeward(): return lax.ppermute(block, 'expert', ways[1 - way])  4.65 us
    pallas_call x1, Pallas kernels, take_inputs_in(): pl.pallas_call(first_kernel, out_shape=[made((rows, hidden_width), jnp.bf...  3.25 us
    pallas_call x1, Pallas kernels, take_output_in(): pl.pallas_call(functools.partial(second_kernel, top_count), out_shape=[ma...  2.18 us
  transfers between devices with their start and end apart: 17, of which 12 were waited for; matrix products, arithmetic and copies ran while one was open for 1% of the time, Pallas kernels for 30%

commit v1 on v0

--- a/solution.py
+++ b/solution.py
@@ -12,7 +12,7 @@
 IN_HBM = pl.BlockSpec(memory_space=pltpu.HBM)
 DEPTH_STEP = 512
 HIDDEN_STEP = 256
-PASS_ROWS = 192
+PASS_ROWS = 256
 SCOPED_BYTES = 8 * 1024 * 1024
 KEPT_BYTES = 32 * 1024 * 1024
 

time: 62.2 us -> 65.4 us (1.051)
  waiting for transfers between devices: 26.5 us -> 23.1 us
  starting transfers between devices: 12.6 us -> 15.9 us
  Pallas kernels: 21.6 us -> 24.9 us
    pallas_call x7, Pallas kernels: 15.1 us -> 18.4 us  [run_experts(): pl.pallas_call(functools.partial(expert_kernel, blocks, flips, bool(prior...]
    ppermute x7, starting transfers between devices: 4.65 us -> 7.8 us  [homeward(): return lax.ppermute(block, 'expert', ways[1 - way])]
    ppermute x7, waiting for transfers between devices: 10.9 us -> 9.11 us  [outward(): return lax.ppermute(block, 'expert', ways[way])]
    ppermute x7, waiting for transfers between devices: 15.6 us -> 14 us  [homeward(): return lax.ppermute(block, 'expert', ways[1 - way])]
  transfers between devices with their start and end apart: 17 -> 17, of which waited for: 12 -> 9; matrix products, arithmetic and copies ran while one was open for 1% -> 1% of each run, Pallas kernels for 30% -> 34%
where the time goes in v1:
time: 65.4 us; the launch traced here: 65.2 us
  Pallas kernels  24.9 us (38%)
  waiting for transfers between devices  23.1 us (35%)
  starting transfers between devices  15.9 us (24%)
  other arithmetic  1.15 us (2%)
    pallas_call x7, Pallas kernels, run_experts(): pl.pallas_call(functools.partial(expert_kernel, blocks, flips, bool(prior...  18.4 us
    ppermute x7, waiting for transfers between devices, homeward(): return lax.ppermute(block, 'expert', ways[1 - way])  14 us
    ppermute x7, waiting for transfers between devices, outward(): return lax.ppermute(block, 'expert', ways[way])  9.11 us
    ppermute x7, starting transfers between devices, homeward(): return lax.ppermute(block, 'expert', ways[1 - way])  7.8 us
    ppermute x7, starting transfers between devices, outward(): return lax.ppermute(block, 'expert', ways[way])  7.16 us
    pallas_call x1, Pallas kernels, take_inputs_in(): pl.pallas_call(first_kernel, out_shape=[made((rows, hidden_width), jnp.bf...  3.25 us
    pallas_call x1, Pallas kernels, take_output_in(): pl.pallas_call(functools.partial(second_kernel, top_count), out_shape=[ma...  2.18 us
  transfers between devices with their start and end apart: 17, of which 9 were waited for; matrix products, arithmetic and copies ran while one was open for 1% of the time, Pallas kernels for 34%

profile of v1, /device:TPU:0, one launch (start us, length us, event | category | flops | bytes accessed | tf_op | source)
XLA Modules:
  0.0 65.2 jit_solution(7044027696476241823)
XLA Ops:
  0.0 0.5 collective-permute-start.7
  0.5 0.1 collective-permute-start.8
  0.5 0.5 collective-permute-start.9
  1.0 1.0 %shard_map.64.rows_ref.refs_1_ = bf16[64,2176]{1,0:T(8,128)(2,1)S(1)} custom-call(bf16[64,2048]{1,0:T(8,128)(2,1)} %tokens_ref.1, s32[8,64]{1,0:T(8,128)} %bitcast.2, f32[8,64]{1,0:T(8,128)} %bitcast.3), custom_call_target="tpu_custom_call" | custom-call | tf_op jit(solution)/shard_map/pallas_call | solution.py:86
  2.0 2.7 %collective-permute-start.1 = (bf16[64,2176]{1,0:T(8,128)(2,1)S(1)}, bf16[64,2176]{1,0:T(8,128)(2,1)S(1)}, u32[]{:S(2)}, u32[]{:S(2)}) collective-permute-start(bf16[64,2176]{1,0:T(8,128)(2,1)S(1)} %shard_map.64.rows_ref.refs_1_), channel_id=1, source_target_pairs={{0,3},{1,4},{2,1},{3,6},{6,11},{7,2},{10,7},{11,14},{14,13},{15,10... | collective-permute-start | bytes 835592 | tf_op jit(solution)/shard_map/ppermute | solution.py:294
  4.7 3.2 %shard_map.65 = (bf16[64,768]{1,0:T(8,128)(2,1)S(1)}, bf16[1,2048,768]{2,1,0:T(8,128)(2,1)S(1)}, bf16[1,2048,768]{2,1,0:T(8,128)(2,1)S(1)}) custom-call(bf16[64,2176]{1,0:T(8,128)(2,1)S(1)} %shard_map.64.rows_ref.refs_1_, bf16[1,2048,768]{2,1,0:T(8,128)(2,1)} %gate_in.1, bf16[1,2048,768]{2,1,0:T(8,128)(2,1)} %up_in.1), custom_call_target="tpu_custom_call" | custom-call | flops 402653184 | bytes 6291456 | tf_op jit(solution)/shard_map/pallas_call | solution.py:219
  7.9 0.1 collective-permute-start
  8.0 2.2 %shard_map.66 = (f32[64,2048]{1,0:T(8,128)S(1)}, bf16[1,768,2048]{2,1,0:T(8,128)(2,1)S(1)}) custom-call(bf16[64,2176]{1,0:T(8,128)(2,1)S(1)} %shard_map.64.rows_ref.refs_1_, bf16[64,768]{1,0:T(8,128)(2,1)S(1)} %get-tuple-element.53.hidden_ref, bf16[1,768,2048]{2,1,0:T(8,128)(2,1)} %down_in.1), custom_call_target="tpu_custom_call" | custom-call | flops 201326592 | bytes 3145728 | tf_op jit(solution)/shard_map/pallas_call | solution.py:241
  10.2 0.0 collective-permute-done.1.refs_0_
  10.2 1.7 %collective-permute-start.3 = (bf16[64,2176]{1,0:T(8,128)(2,1)S(1)}, bf16[64,2176]{1,0:T(8,128)(2,1)S(1)}, u32[]{:S(2)}, u32[]{:S(2)}) collective-permute-start(bf16[64,2176]{1,0:T(8,128)(2,1)S(1)} %collective-permute-done.1.refs_0_), channel_id=1, source_target_pairs={{0,3},{1,4},{2,1},{3,6},{6,11},{7,2},{10,7},{11,14},{14,13},{15,10... | collective-permute-start | bytes 835592 | tf_op jit(solution)/shard_map/ppermute | solution.py:294
  12.0 2.6 %shard_map.67.refs_5_ = f32[64,2048]{1,0:T(8,128)S(1)} custom-call(bf16[64,2176]{1,0:T(8,128)(2,1)S(1)} %collective-permute-done.1.refs_0_, bf16[1,2048,768]{2,1,0:T(8,128)(2,1)S(1)} %get-tuple-element.56.refs_1_.refs_2_, bf16[1,2048,768]{2,1,0:T(8,128)(2,1)S(1)} %get-tuple-element.57.refs_2_.refs_3_, bf16[1,768,2048]{2,1,0:T(8,128)(2,1)S(1)} %get-tuple-element.58.refs_3_.refs_4_), custom_call_target="tpu_custom_call" | custom-call | flops 603979776 | bytes 9961472 | tf_op jit(solution)/shard_map/pallas_call | solution.py:141
  14.6 0.0 collective-permute-done.refs_1_
  14.6 0.1 collective-permute-start.2
  14.7 2.4 %collective-permute-done.3.refs_0_ = bf16[64,2176]{1,0:T(8,128)(2,1)S(1)} collective-permute-done((bf16[64,2176]{1,0:T(8,128)(2,1)S(1)}, bf16[64,2176]{1,0:T(8,128)(2,1)S(1)}, u32[]{:S(2)}, u32[]{:S(2)}) %collective-permute-start.3) | collective-permute-done | bytes 278560 | tf_op jit(solution)/shard_map/ppermute | solution.py:294
  17.2 1.5 %collective-permute-start.5 = (bf16[64,2176]{1,0:T(8,128)(2,1)S(1)}, bf16[64,2176]{1,0:T(8,128)(2,1)S(1)}, u32[]{:S(2)}, u32[]{:S(2)}) collective-permute-start(bf16[64,2176]{1,0:T(8,128)(2,1)S(1)} %collective-permute-done.3.refs_0_), channel_id=1, source_target_pairs={{0,3},{1,4},{2,1},{3,6},{6,11},{7,2},{10,7},{11,14},{14,13},{15,10... | collective-permute-start | bytes 835592 | tf_op jit(solution)/shard_map/ppermute | solution.py:294
  18.7 2.6 %shard_map.68 = (f32[64,2048]{1,0:T(8,128)S(1)}, f32[64,2048]{1,0:T(8,128)S(1)}) custom-call(bf16[64,2176]{1,0:T(8,128)(2,1)S(1)} %collective-permute-done.3.refs_0_, bf16[64,2176]{1,0:T(8,128)(2,1)S(1)} %collective-permute-done.refs_1_, bf16[1,2048,768]{2,1,0:T(8,128)(2,1)S(1)} %get-tuple-element.56.refs_1_.refs_2_, ...), custom_call_target="tpu_custom_call" | custom-call | flops 1207959552 | bytes 10485760 | tf_op jit(solution)/shard_map/pallas_call | solution.py:141
  21.3 0.0 collective-permute-done.2.refs_1_
  21.3 0.3 collective-permute-start.4
  21.6 2.7 %collective-permute-done.5.refs_0_ = bf16[64,2176]{1,0:T(8,128)(2,1)S(1)} collective-permute-done((bf16[64,2176]{1,0:T(8,128)(2,1)S(1)}, bf16[64,2176]{1,0:T(8,128)(2,1)S(1)}, u32[]{:S(2)}, u32[]{:S(2)}) %collective-permute-start.5) | collective-permute-done | bytes 278560 | tf_op jit(solution)/shard_map/ppermute | solution.py:294
  24.3 0.7 %collective-permute-start.6 = (bf16[64,2176]{1,0:T(8,128)(2,1)S(1)}, bf16[64,2176]{1,0:T(8,128)(2,1)S(1)}, u32[]{:S(2)}, u32[]{:S(2)}) collective-permute-start(bf16[64,2176]{1,0:T(8,128)(2,1)S(1)} %collective-permute-done.5.refs_0_), channel_id=1, source_target_pairs={{0,3},{1,4},{2,1},{3,6},{6,11},{7,2},{10,7},{11,14},{14,13},{15,10... | collective-permute-start | bytes 835592 | tf_op jit(solution)/shard_map/ppermute | solution.py:294
  25.0 2.6 %shard_map.69 = (f32[64,2048]{1,0:T(8,128)S(1)}, f32[64,2048]{1,0:T(8,128)S(1)}) custom-call(bf16[64,2176]{1,0:T(8,128)(2,1)S(1)} %collective-permute-done.5.refs_0_, bf16[64,2176]{1,0:T(8,128)(2,1)S(1)} %collective-permute-done.2.refs_1_, bf16[1,2048,768]{2,1,0:T(8,128)(2,1)S(1)} %get-tuple-element.56.refs_1_.refs_2_, ...), custom_call_target="tpu_custom_call" | custom-call | flops 1207959552 | bytes 10485760 | tf_op jit(solution)/shard_map/pallas_call | solution.py:141
  27.6 0.5 collective-permute-done.4.refs_0_
  28.1 3.5 %collective-permute-done.6.refs_1_ = bf16[64,2176]{1,0:T(8,128)(2,1)S(1)} collective-permute-done((bf16[64,2176]{1,0:T(8,128)(2,1)S(1)}, bf16[64,2176]{1,0:T(8,128)(2,1)S(1)}, u32[]{:S(2)}, u32[]{:S(2)}) %collective-permute-start.6) | collective-permute-done | bytes 278560 | tf_op jit(solution)/shard_map/ppermute | solution.py:294
  31.6 0.0 collective-permute-done.7.refs_5_.refs_2_
  31.6 0.0 collective-permute-done.8.refs_6_.refs_3_
  31.6 0.0 collective-permute-done.9.refs_7_.refs_4_
  31.6 2.8 %shard_map.70 = (f32[64,2048]{1,0:T(8,128)S(1)}, f32[64,2048]{1,0:T(8,128)S(1)}) custom-call(bf16[64,2176]{1,0:T(8,128)(2,1)S(1)} %collective-permute-done.4.refs_0_, bf16[64,2176]{1,0:T(8,128)(2,1)S(1)} %collective-permute-done.6.refs_1_, bf16[1,2048,768]{2,1,0:T(8,128)(2,1)S(1)} %get-tuple-element.56.refs_1_.refs_2_, ...), custom_call_target="tpu_custom_call" | custom-call | flops 2415919104 | bytes 19922944 | tf_op jit(solution)/shard_map/pallas_call | solution.py:141
  34.4 0.4 collective-permute-start.11
  34.8 2.6 %shard_map.71 = (f32[64,2048]{1,0:T(8,128)S(1)}, f32[64,2048]{1,0:T(8,128)S(1)}) custom-call(bf16[64,2176]{1,0:T(8,128)(2,1)S(1)} %collective-permute-done.5.refs_0_, bf16[64,2176]{1,0:T(8,128)(2,1)S(1)} %collective-permute-done.2.refs_1_, bf16[1,2048,768]{2,1,0:T(8,128)(2,1)S(1)} %collective-permute-done.7.refs_5_.refs_2_, ...), custom_call_target="tpu_custom_call" | custom-call | flops 1207959552 | bytes 10485760 | tf_op jit(solution)/shard_map/pallas_call | solution.py:141
  37.5 1.6 %collective-permute-start.10 = (bf16[64,2048]{1,0:T(8,128)(2,1)S(1)}, bf16[64,2048]{1,0:T(8,128)(2,1)S(1)}, u32[]{:S(2)}, u32[]{:S(2)}) collective-permute-start(bf16[64,2048]{1,0:T(8,128)(2,1)S(1)} %convert_element_type.46), channel_id=1, source_target_pairs={{0,3},{1,4},{2,1},{3,6},{6,11},{7,2},{10,7},{11,14},{14,13},{15,10... | collective-permute-start | bytes 786440 | tf_op jit(solution)/shard_map/ppermute | solution.py:297
  39.1 1.3 %collective-permute-done.11 = bf16[64,2048]{1,0:T(8,128)(2,1)S(1)} collective-permute-done((bf16[64,2048]{1,0:T(8,128)(2,1)S(1)}, bf16[64,2048]{1,0:T(8,128)(2,1)S(1)}, u32[]{:S(2)}, u32[]{:S(2)}) %collective-permute-start.11) | collective-permute-done | bytes 262176 | tf_op jit(solution)/shard_map/ppermute | solution.py:297
  40.5 1.1 %collective-permute-start.13 = (bf16[64,2048]{1,0:T(8,128)(2,1)S(1)}, bf16[64,2048]{1,0:T(8,128)(2,1)S(1)}, u32[]{:S(2)}, u32[]{:S(2)}) collective-permute-start(bf16[64,2048]{1,0:T(8,128)(2,1)S(1)} %add_convert_fusion.5), channel_id=1, source_target_pairs={{0,5},{1,2},{2,7},{3,0},{6,3},{7,10},{10,15},{11,6},{14,11},{15,12... | collective-permute-start | bytes 786440 | tf_op jit(solution)/shard_map/ppermute | solution.py:297
  41.6 2.6 %shard_map.72 = (f32[64,2048]{1,0:T(8,128)S(1)}, f32[64,2048]{1,0:T(8,128)S(1)}) custom-call(bf16[64,2176]{1,0:T(8,128)(2,1)S(1)} %collective-permute-done.3.refs_0_, bf16[64,2176]{1,0:T(8,128)(2,1)S(1)} %collective-permute-done.refs_1_, bf16[1,2048,768]{2,1,0:T(8,128)(2,1)S(1)} %collective-permute-done.7.refs_5_.refs_2_, ...), custom_call_target="tpu_custom_call" | custom-call | flops 1207959552 | bytes 10485760 | tf_op jit(solution)/shard_map/pallas_call | solution.py:141
  44.2 0.9 %collective-permute-done.10 = bf16[64,2048]{1,0:T(8,128)(2,1)S(1)} collective-permute-done((bf16[64,2048]{1,0:T(8,128)(2,1)S(1)}, bf16[64,2048]{1,0:T(8,128)(2,1)S(1)}, u32[]{:S(2)}, u32[]{:S(2)}) %collective-permute-start.10) | collective-permute-done | bytes 262176 | tf_op jit(solution)/shard_map/ppermute | solution.py:297
  45.1 0.1 add_convert_fusion.4
  45.2 0.6 collective-permute-start.12
  45.8 2.0 %collective-permute-done.13 = bf16[64,2048]{1,0:T(8,128)(2,1)S(1)} collective-permute-done((bf16[64,2048]{1,0:T(8,128)(2,1)S(1)}, bf16[64,2048]{1,0:T(8,128)(2,1)S(1)}, u32[]{:S(2)}, u32[]{:S(2)}) %collective-permute-start.13) | collective-permute-done | bytes 262176 | tf_op jit(solution)/shard_map/ppermute | solution.py:297
  47.7 0.1 add_convert_fusion.3
  47.8 1.4 %collective-permute-start.15 = (bf16[64,2048]{1,0:T(8,128)(2,1)S(1)}, bf16[64,2048]{1,0:T(8,128)(2,1)S(1)}, u32[]{:S(2)}, u32[]{:S(2)}) collective-permute-start(bf16[64,2048]{1,0:T(8,128)(2,1)S(1)} %add_convert_fusion.3), channel_id=1, source_target_pairs={{0,5},{1,2},{2,7},{3,0},{6,3},{7,10},{10,15},{11,6},{14,11},{15,12... | collective-permute-start | bytes 786440 | tf_op jit(solution)/shard_map/ppermute | solution.py:297
  49.2 2.6 %shard_map.73 = (f32[64,2048]{1,0:T(8,128)S(1)}, f32[64,2048]{1,0:T(8,128)S(1)}) custom-call(bf16[64,2176]{1,0:T(8,128)(2,1)S(1)} %collective-permute-done.1.refs_0_, bf16[64,2176]{1,0:T(8,128)(2,1)S(1)} %shard_map.64.rows_ref.refs_1_, bf16[1,2048,768]{2,1,0:T(8,128)(2,1)S(1)} %collective-permute-done.7.refs_5_.refs_2_, ...), custom_call_target="tpu_custom_call" | custom-call | flops 1207959552 | bytes 10485760 | tf_op jit(solution)/shard_map/pallas_call | solution.py:141
  51.8 3.4 %collective-permute-done.12 = bf16[64,2048]{1,0:T(8,128)(2,1)S(1)} collective-permute-done((bf16[64,2048]{1,0:T(8,128)(2,1)S(1)}, bf16[64,2048]{1,0:T(8,128)(2,1)S(1)}, u32[]{:S(2)}, u32[]{:S(2)}) %collective-permute-start.12) | collective-permute-done | bytes 262176 | tf_op jit(solution)/shard_map/ppermute | solution.py:297
  55.2 0.1 add_convert_fusion.2
  55.2 0.1 collective-permute-start.14
  55.3 0.0 collective-permute-done.15
  55.4 2.7 %collective-permute-start.16 = (bf16[64,2048]{1,0:T(8,128)(2,1)S(1)}, bf16[64,2048]{1,0:T(8,128)(2,1)S(1)}, u32[]{:S(2)}, u32[]{:S(2)}) collective-permute-start(bf16[64,2048]{1,0:T(8,128)(2,1)S(1)} %add_convert_fusion.1), channel_id=1, source_target_pairs={{0,5},{1,2},{2,7},{3,0},{6,3},{7,10},{10,15},{11,6},{14,11},{15,12... | collective-permute-start | bytes 786440 | tf_op jit(solution)/shard_map/ppermute | solution.py:297
  58.0 6.4 %collective-permute-done.14 = bf16[64,2048]{1,0:T(8,128)(2,1)S(1)} collective-permute-done((bf16[64,2048]{1,0:T(8,128)(2,1)S(1)}, bf16[64,2048]{1,0:T(8,128)(2,1)S(1)}, u32[]{:S(2)}, u32[]{:S(2)}) %collective-permute-start.14) | collective-permute-done | bytes 262176 | tf_op jit(solution)/shard_map/ppermute | solution.py:297
  64.4 0.1 convert_add_fusion
  64.5 0.0 collective-permute-done.16
  64.5 0.8 %add_convert_fusion = bf16[64,2048]{1,0:T(8,128)(2,1)} fusion(f32[64,2048]{1,0:T(8,128)S(1)} %convert_add_fusion, bf16[64,2048]{1,0:T(8,128)(2,1)S(1)} %collective-permute-done.16), kind=kLoop, calls=%fused_computation | loop fusion | flops 393216 | bytes 1048576 | tf_op jit(solution)/shard_map/convert_element_type | solution.py:275
  (4 shorter events, 0.2 us)
Async XLA Ops:
  0.0 31.6 %collective-permute-start.7 = (bf16[1,2048,768]{2,1,0:T(8,128)(2,1)}, bf16[1,2048,768]{2,1,0:T(8,128)(2,1)S(1)}, u32[]{:S(2)}, u32[]{:S(2)}) collective-permute-start(bf16[1,2048,768]{2,1,0:T(8,128)(2,1)} %gate_in.1), channel_id=1, source_target_pairs={{0,1},{1,0},{2,3},{3,2},{4,5},{5,4},{6,7},{7,6},{8,9},{9,8},{10,11... | collective-permute-start | bytes 9437192 | tf_op jit(solution)/shard_map/ppermute | solution.py:300
  0.5 31.1 %collective-permute-start.8 = (bf16[1,2048,768]{2,1,0:T(8,128)(2,1)}, bf16[1,2048,768]{2,1,0:T(8,128)(2,1)S(1)}, u32[]{:S(2)}, u32[]{:S(2)}) collective-permute-start(bf16[1,2048,768]{2,1,0:T(8,128)(2,1)} %up_in.1), channel_id=1, source_target_pairs={{0,1},{1,0},{2,3},{3,2},{4,5},{5,4},{6,7},{7,6},{8,9},{9,8},{10,11... | collective-permute-start | bytes 9437192 | tf_op jit(solution)/shard_map/ppermute | solution.py:300
  0.5 31.1 %collective-permute-start.9 = (bf16[1,768,2048]{2,1,0:T(8,128)(2,1)}, bf16[1,768,2048]{2,1,0:T(8,128)(2,1)S(1)}, u32[]{:S(2)}, u32[]{:S(2)}) collective-permute-start(bf16[1,768,2048]{2,1,0:T(8,128)(2,1)} %down_in.1), channel_id=1, source_target_pairs={{0,1},{1,0},{2,3},{3,2},{4,5},{5,4},{6,7},{7,6},{8,9},{9,8},{10,11... | collective-permute-start | bytes 9437192 | tf_op jit(solution)/shard_map/ppermute | solution.py:300
  2.0 8.3 %collective-permute-start.1 = (bf16[64,2176]{1,0:T(8,128)(2,1)S(1)}, bf16[64,2176]{1,0:T(8,128)(2,1)S(1)}, u32[]{:S(2)}, u32[]{:S(2)}) collective-permute-start(bf16[64,2176]{1,0:T(8,128)(2,1)S(1)} %shard_map.64.rows_ref.refs_1_), channel_id=1, source_target_pairs={{0,3},{1,4},{2,1},{3,6},{6,11},{7,2},{10,7},{11,14},{14,13},{15,10... | collective-permute-start | bytes 835592 | tf_op jit(solution)/shard_map/ppermute | solution.py:294
  7.9 6.7 %collective-permute-start = (bf16[64,2176]{1,0:T(8,128)(2,1)S(1)}, bf16[64,2176]{1,0:T(8,128)(2,1)S(1)}, u32[]{:S(2)}, u32[]{:S(2)}) collective-permute-start(bf16[64,2176]{1,0:T(8,128)(2,1)S(1)} %shard_map.64.rows_ref.refs_1_), channel_id=1, source_target_pairs={{0,5},{1,2},{2,7},{3,0},{6,3},{7,10},{10,15},{11,6},{14,11},{15,12... | collective-permute-start | bytes 835592 | tf_op jit(solution)/shard_map/ppermute | solution.py:294
  10.2 6.9 %collective-permute-start.3 = (bf16[64,2176]{1,0:T(8,128)(2,1)S(1)}, bf16[64,2176]{1,0:T(8,128)(2,1)S(1)}, u32[]{:S(2)}, u32[]{:S(2)}) collective-permute-start(bf16[64,2176]{1,0:T(8,128)(2,1)S(1)} %collective-permute-done.1.refs_0_), channel_id=1, source_target_pairs={{0,3},{1,4},{2,1},{3,6},{6,11},{7,2},{10,7},{11,14},{14,13},{15,10... | collective-permute-start | bytes 835592 | tf_op jit(solution)/shard_map/ppermute | solution.py:294
  14.6 6.7 %collective-permute-start.2 = (bf16[64,2176]{1,0:T(8,128)(2,1)S(1)}, bf16[64,2176]{1,0:T(8,128)(2,1)S(1)}, u32[]{:S(2)}, u32[]{:S(2)}) collective-permute-start(bf16[64,2176]{1,0:T(8,128)(2,1)S(1)} %collective-permute-done.refs_1_), channel_id=1, source_target_pairs={{0,5},{1,2},{2,7},{3,0},{6,3},{7,10},{10,15},{11,6},{14,11},{15,12... | collective-permute-start | bytes 835592 | tf_op jit(solution)/shard_map/ppermute | solution.py:294
  17.2 7.1 %collective-permute-start.5 = (bf16[64,2176]{1,0:T(8,128)(2,1)S(1)}, bf16[64,2176]{1,0:T(8,128)(2,1)S(1)}, u32[]{:S(2)}, u32[]{:S(2)}) collective-permute-start(bf16[64,2176]{1,0:T(8,128)(2,1)S(1)} %collective-permute-done.3.refs_0_), channel_id=1, source_target_pairs={{0,3},{1,4},{2,1},{3,6},{6,11},{7,2},{10,7},{11,14},{14,13},{15,10... | collective-permute-start | bytes 835592 | tf_op jit(solution)/shard_map/ppermute | solution.py:294
  21.3 6.8 %collective-permute-start.4 = (bf16[64,2176]{1,0:T(8,128)(2,1)S(1)}, bf16[64,2176]{1,0:T(8,128)(2,1)S(1)}, u32[]{:S(2)}, u32[]{:S(2)}) collective-permute-start(bf16[64,2176]{1,0:T(8,128)(2,1)S(1)} %collective-permute-done.2.refs_1_), channel_id=1, source_target_pairs={{0,5},{1,2},{2,7},{3,0},{6,3},{7,10},{10,15},{11,6},{14,11},{15,12... | collective-permute-start | bytes 835592 | tf_op jit(solution)/shard_map/ppermute | solution.py:294
  24.3 7.3 %collective-permute-start.6 = (bf16[64,2176]{1,0:T(8,128)(2,1)S(1)}, bf16[64,2176]{1,0:T(8,128)(2,1)S(1)}, u32[]{:S(2)}, u32[]{:S(2)}) collective-permute-start(bf16[64,2176]{1,0:T(8,128)(2,1)S(1)} %collective-permute-done.5.refs_0_), channel_id=1, source_target_pairs={{0,3},{1,4},{2,1},{3,6},{6,11},{7,2},{10,7},{11,14},{14,13},{15,10... | collective-permute-start | bytes 835592 | tf_op jit(solution)/shard_map/ppermute | solution.py:294
  34.4 6.0 %collective-permute-start.11 = (bf16[64,2048]{1,0:T(8,128)(2,1)S(1)}, bf16[64,2048]{1,0:T(8,128)(2,1)S(1)}, u32[]{:S(2)}, u32[]{:S(2)}) collective-permute-start(bf16[64,2048]{1,0:T(8,128)(2,1)S(1)} %convert_element_type.45), channel_id=1, source_target_pairs={{0,5},{1,2},{2,7},{3,0},{6,3},{7,10},{10,15},{11,6},{14,11},{15,12... | collective-permute-start | bytes 786440 | tf_op jit(solution)/shard_map/ppermute | solution.py:297
  37.5 7.6 %collective-permute-start.10 = (bf16[64,2048]{1,0:T(8,128)(2,1)S(1)}, bf16[64,2048]{1,0:T(8,128)(2,1)S(1)}, u32[]{:S(2)}, u32[]{:S(2)}) collective-permute-start(bf16[64,2048]{1,0:T(8,128)(2,1)S(1)} %convert_element_type.46), channel_id=1, source_target_pairs={{0,3},{1,4},{2,1},{3,6},{6,11},{7,2},{10,7},{11,14},{14,13},{15,10... | collective-permute-start | bytes 786440 | tf_op jit(solution)/shard_map/ppermute | solution.py:297
  40.5 7.2 %collective-permute-start.13 = (bf16[64,2048]{1,0:T(8,128)(2,1)S(1)}, bf16[64,2048]{1,0:T(8,128)(2,1)S(1)}, u32[]{:S(2)}, u32[]{:S(2)}) collective-permute-start(bf16[64,2048]{1,0:T(8,128)(2,1)S(1)} %add_convert_fusion.5), channel_id=1, source_target_pairs={{0,5},{1,2},{2,7},{3,0},{6,3},{7,10},{10,15},{11,6},{14,11},{15,12... | collective-permute-start | bytes 786440 | tf_op jit(solution)/shard_map/ppermute | solution.py:297
  45.2 10.0 %collective-permute-start.12 = (bf16[64,2048]{1,0:T(8,128)(2,1)S(1)}, bf16[64,2048]{1,0:T(8,128)(2,1)S(1)}, u32[]{:S(2)}, u32[]{:S(2)}) collective-permute-start(bf16[64,2048]{1,0:T(8,128)(2,1)S(1)} %add_convert_fusion.4), channel_id=1, source_target_pairs={{0,3},{1,4},{2,1},{3,6},{6,11},{7,2},{10,7},{11,14},{14,13},{15,10... | collective-permute-start | bytes 786440 | tf_op jit(solution)/shard_map/ppermute | solution.py:297
  47.8 7.5 %collective-permute-start.15 = (bf16[64,2048]{1,0:T(8,128)(2,1)S(1)}, bf16[64,2048]{1,0:T(8,128)(2,1)S(1)}, u32[]{:S(2)}, u32[]{:S(2)}) collective-permute-start(bf16[64,2048]{1,0:T(8,128)(2,1)S(1)} %add_convert_fusion.3), channel_id=1, source_target_pairs={{0,5},{1,2},{2,7},{3,0},{6,3},{7,10},{10,15},{11,6},{14,11},{15,12... | collective-permute-start | bytes 786440 | tf_op jit(solution)/shard_map/ppermute | solution.py:297
  55.2 9.2 %collective-permute-start.14 = (bf16[64,2048]{1,0:T(8,128)(2,1)S(1)}, bf16[64,2048]{1,0:T(8,128)(2,1)S(1)}, u32[]{:S(2)}, u32[]{:S(2)}) collective-permute-start(bf16[64,2048]{1,0:T(8,128)(2,1)S(1)} %add_convert_fusion.2), channel_id=1, source_target_pairs={{0,3},{1,4},{2,1},{3,6},{6,11},{7,2},{10,7},{11,14},{14,13},{15,10... | collective-permute-start | bytes 786440 | tf_op jit(solution)/shard_map/ppermute | solution.py:297
  55.4 9.1 %collective-permute-start.16 = (bf16[64,2048]{1,0:T(8,128)(2,1)S(1)}, bf16[64,2048]{1,0:T(8,128)(2,1)S(1)}, u32[]{:S(2)}, u32[]{:S(2)}) collective-permute-start(bf16[64,2048]{1,0:T(8,128)(2,1)S(1)} %add_convert_fusion.1), channel_id=1, source_target_pairs={{0,5},{1,2},{2,7},{3,0},{6,3},{7,10},{10,15},{11,6},{14,11},{15,12... | collective-permute-start | bytes 786440 | tf_op jit(solution)/shard_map/ppermute | solution.py:297

commit v2 on v0

--- a/solution.py
+++ b/solution.py
@@ -45,7 +45,7 @@
     pairs = []
     for at, chip in enumerate(ring):
         for core in (0, 1):
-            step = way if core == at % 2 else -way
+            step = -way if core == at % 2 else way
             pairs.append((2 * chip + core, 2 * ring[(at + step) % count] + 1 - core))
     return pairs
 

time: 62.2 us -> 62.7 us (level)
  starting transfers between devices: 12.6 us -> 13.4 us
    ppermute x7, waiting for transfers between devices: 10.9 us -> 10.1 us  [outward(): return lax.ppermute(block, 'expert', ways[way])]
    ppermute x7, starting transfers between devices: 7.04 us -> 7.69 us  [outward(): return lax.ppermute(block, 'expert', ways[way])]
where the time goes in v2:
time: 62.7 us; the launch traced here: 62.5 us
  waiting for transfers between devices  26.2 us (42%)
  Pallas kernels  21.6 us (34%)
  starting transfers between devices  13.4 us (21%)
  other arithmetic  1.15 us (2%)
    ppermute x7, waiting for transfers between devices, homeward(): return lax.ppermute(block, 'expert', ways[1 - way])  16.1 us
    pallas_call x7, Pallas kernels, run_experts(): pl.pallas_call(functools.partial(expert_kernel, blocks, flips, bool(prior...  15.1 us
    ppermute x7, waiting for transfers between devices, outward(): return lax.ppermute(block, 'expert', ways[way])  10.1 us
    ppermute x7, starting transfers between devices, outward(): return lax.ppermute(block, 'expert', ways[way])  7.69 us
    ppermute x7, starting transfers between devices, homeward(): return lax.ppermute(block, 'expert', ways[1 - way])  4.75 us
    pallas_call x1, Pallas kernels, take_inputs_in(): pl.pallas_call(first_kernel, out_shape=[made((rows, hidden_width), jnp.bf...  3.25 us
    pallas_call x1, Pallas kernels, take_output_in(): pl.pallas_call(functools.partial(second_kernel, top_count), out_shape=[ma...  2.19 us
  transfers between devices with their start and end apart: 17, of which 12 were waited for; matrix products, arithmetic and copies ran while one was open for 1% of the time, Pallas kernels for 30%

profile of v2, /device:TPU:0, one launch (start us, length us, event | category | flops | bytes accessed | tf_op | source)
XLA Modules:
  0.0 62.5 jit_solution(2981558179495527767)
XLA Ops:
  0.0 0.5 collective-permute-start.7
  0.5 0.1 collective-permute-start.8
  0.5 0.5 collective-permute-start.9
  1.0 1.0 %shard_map.64.rows_ref.refs_1_ = bf16[64,2176]{1,0:T(8,128)(2,1)S(1)} custom-call(bf16[64,2048]{1,0:T(8,128)(2,1)} %tokens_ref.1, s32[8,64]{1,0:T(8,128)} %bitcast.2, f32[8,64]{1,0:T(8,128)} %bitcast.3), custom_call_target="tpu_custom_call" | custom-call | tf_op jit(solution)/shard_map/pallas_call | solution.py:86
  2.0 2.7 %collective-permute-start.1 = (bf16[64,2176]{1,0:T(8,128)(2,1)S(1)}, bf16[64,2176]{1,0:T(8,128)(2,1)S(1)}, u32[]{:S(2)}, u32[]{:S(2)}) collective-permute-start(bf16[64,2176]{1,0:T(8,128)(2,1)S(1)} %shard_map.64.rows_ref.refs_1_), channel_id=1, source_target_pairs={{0,5},{1,2},{2,7},{3,0},{6,3},{7,10},{10,15},{11,6},{14,11},{15,12... | collective-permute-start | bytes 835592 | tf_op jit(solution)/shard_map/ppermute | solution.py:294
  4.7 3.2 %shard_map.65 = (bf16[64,768]{1,0:T(8,128)(2,1)S(1)}, bf16[1,2048,768]{2,1,0:T(8,128)(2,1)S(1)}, bf16[1,2048,768]{2,1,0:T(8,128)(2,1)S(1)}) custom-call(bf16[64,2176]{1,0:T(8,128)(2,1)S(1)} %shard_map.64.rows_ref.refs_1_, bf16[1,2048,768]{2,1,0:T(8,128)(2,1)} %gate_in.1, bf16[1,2048,768]{2,1,0:T(8,128)(2,1)} %up_in.1), custom_call_target="tpu_custom_call" | custom-call | flops 402653184 | bytes 6291456 | tf_op jit(solution)/shard_map/pallas_call | solution.py:219
  8.0 0.1 collective-permute-start
  8.0 2.2 %shard_map.66 = (f32[64,2048]{1,0:T(8,128)S(1)}, bf16[1,768,2048]{2,1,0:T(8,128)(2,1)S(1)}) custom-call(bf16[64,2176]{1,0:T(8,128)(2,1)S(1)} %shard_map.64.rows_ref.refs_1_, bf16[64,768]{1,0:T(8,128)(2,1)S(1)} %get-tuple-element.53.hidden_ref, bf16[1,768,2048]{2,1,0:T(8,128)(2,1)} %down_in.1), custom_call_target="tpu_custom_call" | custom-call | flops 201326592 | bytes 3145728 | tf_op jit(solution)/shard_map/pallas_call | solution.py:241
  10.2 0.0 collective-permute-done.1.refs_0_
  10.2 1.8 %collective-permute-start.3 = (bf16[64,2176]{1,0:T(8,128)(2,1)S(1)}, bf16[64,2176]{1,0:T(8,128)(2,1)S(1)}, u32[]{:S(2)}, u32[]{:S(2)}) collective-permute-start(bf16[64,2176]{1,0:T(8,128)(2,1)S(1)} %collective-permute-done.1.refs_0_), channel_id=1, source_target_pairs={{0,5},{1,2},{2,7},{3,0},{6,3},{7,10},{10,15},{11,6},{14,11},{15,12... | collective-permute-start | bytes 835592 | tf_op jit(solution)/shard_map/ppermute | solution.py:294
  12.0 2.0 %shard_map.67.refs_5_ = f32[64,2048]{1,0:T(8,128)S(1)} custom-call(bf16[64,2176]{1,0:T(8,128)(2,1)S(1)} %collective-permute-done.1.refs_0_, bf16[1,2048,768]{2,1,0:T(8,128)(2,1)S(1)} %get-tuple-element.56.refs_1_.refs_2_, bf16[1,2048,768]{2,1,0:T(8,128)(2,1)S(1)} %get-tuple-element.57.refs_2_.refs_3_, bf16[1,768,2048]{2,1,0:T(8,128)(2,1)S(1)} %get-tuple-element.58.refs_3_.refs_4_), custom_call_target="tpu_custom_call" | custom-call | flops 603979776 | bytes 9961472 | tf_op jit(solution)/shard_map/pallas_call | solution.py:141
  14.1 0.4 collective-permute-done.refs_1_
  14.5 0.0 collective-permute-start.2
  14.5 2.7 %collective-permute-done.3.refs_0_ = bf16[64,2176]{1,0:T(8,128)(2,1)S(1)} collective-permute-done((bf16[64,2176]{1,0:T(8,128)(2,1)S(1)}, bf16[64,2176]{1,0:T(8,128)(2,1)S(1)}, u32[]{:S(2)}, u32[]{:S(2)}) %collective-permute-start.3) | collective-permute-done | bytes 278560 | tf_op jit(solution)/shard_map/ppermute | solution.py:294
  17.1 1.8 %collective-permute-start.5 = (bf16[64,2176]{1,0:T(8,128)(2,1)S(1)}, bf16[64,2176]{1,0:T(8,128)(2,1)S(1)}, u32[]{:S(2)}, u32[]{:S(2)}) collective-permute-start(bf16[64,2176]{1,0:T(8,128)(2,1)S(1)} %collective-permute-done.3.refs_0_), channel_id=1, source_target_pairs={{0,5},{1,2},{2,7},{3,0},{6,3},{7,10},{10,15},{11,6},{14,11},{15,12... | collective-permute-start | bytes 835592 | tf_op jit(solution)/shard_map/ppermute | solution.py:294
  18.9 2.1 %shard_map.68 = (f32[64,2048]{1,0:T(8,128)S(1)}, f32[64,2048]{1,0:T(8,128)S(1)}) custom-call(bf16[64,2176]{1,0:T(8,128)(2,1)S(1)} %collective-permute-done.3.refs_0_, bf16[64,2176]{1,0:T(8,128)(2,1)S(1)} %collective-permute-done.refs_1_, bf16[1,2048,768]{2,1,0:T(8,128)(2,1)S(1)} %get-tuple-element.56.refs_1_.refs_2_, ...), custom_call_target="tpu_custom_call" | custom-call | flops 1207959552 | bytes 10485760 | tf_op jit(solution)/shard_map/pallas_call | solution.py:141
  21.0 0.0 collective-permute-done.2.refs_1_
  21.0 0.1 collective-permute-start.4
  21.0 3.1 %collective-permute-done.5.refs_0_ = bf16[64,2176]{1,0:T(8,128)(2,1)S(1)} collective-permute-done((bf16[64,2176]{1,0:T(8,128)(2,1)S(1)}, bf16[64,2176]{1,0:T(8,128)(2,1)S(1)}, u32[]{:S(2)}, u32[]{:S(2)}) %collective-permute-start.5) | collective-permute-done | bytes 278560 | tf_op jit(solution)/shard_map/ppermute | solution.py:294
  24.2 1.3 %collective-permute-start.6 = (bf16[64,2176]{1,0:T(8,128)(2,1)S(1)}, bf16[64,2176]{1,0:T(8,128)(2,1)S(1)}, u32[]{:S(2)}, u32[]{:S(2)}) collective-permute-start(bf16[64,2176]{1,0:T(8,128)(2,1)S(1)} %collective-permute-done.5.refs_0_), channel_id=1, source_target_pairs={{0,5},{1,2},{2,7},{3,0},{6,3},{7,10},{10,15},{11,6},{14,11},{15,12... | collective-permute-start | bytes 835592 | tf_op jit(solution)/shard_map/ppermute | solution.py:294
  25.4 2.0 %shard_map.69 = (f32[64,2048]{1,0:T(8,128)S(1)}, f32[64,2048]{1,0:T(8,128)S(1)}) custom-call(bf16[64,2176]{1,0:T(8,128)(2,1)S(1)} %collective-permute-done.5.refs_0_, bf16[64,2176]{1,0:T(8,128)(2,1)S(1)} %collective-permute-done.2.refs_1_, bf16[1,2048,768]{2,1,0:T(8,128)(2,1)S(1)} %get-tuple-element.56.refs_1_.refs_2_, ...), custom_call_target="tpu_custom_call" | custom-call | flops 1207959552 | bytes 10485760 | tf_op jit(solution)/shard_map/pallas_call | solution.py:141
  27.5 0.7 %collective-permute-done.4.refs_0_ = bf16[64,2176]{1,0:T(8,128)(2,1)S(1)} collective-permute-done((bf16[64,2176]{1,0:T(8,128)(2,1)S(1)}, bf16[64,2176]{1,0:T(8,128)(2,1)S(1)}, u32[]{:S(2)}, u32[]{:S(2)}) %collective-permute-start.4) | collective-permute-done | bytes 278560 | tf_op jit(solution)/shard_map/ppermute | solution.py:294
  28.1 3.3 %collective-permute-done.6.refs_1_ = bf16[64,2176]{1,0:T(8,128)(2,1)S(1)} collective-permute-done((bf16[64,2176]{1,0:T(8,128)(2,1)S(1)}, bf16[64,2176]{1,0:T(8,128)(2,1)S(1)}, u32[]{:S(2)}, u32[]{:S(2)}) %collective-permute-start.6) | collective-permute-done | bytes 278560 | tf_op jit(solution)/shard_map/ppermute | solution.py:294
  31.4 0.0 collective-permute-done.7.refs_5_.refs_2_
  31.4 0.0 collective-permute-done.8.refs_6_.refs_3_
  31.4 0.0 collective-permute-done.9.refs_7_.refs_4_
  31.4 2.8 %shard_map.70 = (f32[64,2048]{1,0:T(8,128)S(1)}, f32[64,2048]{1,0:T(8,128)S(1)}) custom-call(bf16[64,2176]{1,0:T(8,128)(2,1)S(1)} %collective-permute-done.4.refs_0_, bf16[64,2176]{1,0:T(8,128)(2,1)S(1)} %collective-permute-done.6.refs_1_, bf16[1,2048,768]{2,1,0:T(8,128)(2,1)S(1)} %get-tuple-element.56.refs_1_.refs_2_, ...), custom_call_target="tpu_custom_call" | custom-call | flops 2415919104 | bytes 19922944 | tf_op jit(solution)/shard_map/pallas_call | solution.py:141
  34.3 0.5 collective-permute-start.11
  34.8 2.1 %shard_map.71 = (f32[64,2048]{1,0:T(8,128)S(1)}, f32[64,2048]{1,0:T(8,128)S(1)}) custom-call(bf16[64,2176]{1,0:T(8,128)(2,1)S(1)} %collective-permute-done.5.refs_0_, bf16[64,2176]{1,0:T(8,128)(2,1)S(1)} %collective-permute-done.2.refs_1_, bf16[1,2048,768]{2,1,0:T(8,128)(2,1)S(1)} %collective-permute-done.7.refs_5_.refs_2_, ...), custom_call_target="tpu_custom_call" | custom-call | flops 1207959552 | bytes 10485760 | tf_op jit(solution)/shard_map/pallas_call | solution.py:141
  36.9 1.5 %collective-permute-start.10 = (bf16[64,2048]{1,0:T(8,128)(2,1)S(1)}, bf16[64,2048]{1,0:T(8,128)(2,1)S(1)}, u32[]{:S(2)}, u32[]{:S(2)}) collective-permute-start(bf16[64,2048]{1,0:T(8,128)(2,1)S(1)} %convert_element_type.46), channel_id=1, source_target_pairs={{0,5},{1,2},{2,7},{3,0},{6,3},{7,10},{10,15},{11,6},{14,11},{15,12... | collective-permute-start | bytes 786440 | tf_op jit(solution)/shard_map/ppermute | solution.py:297
  38.4 1.9 %collective-permute-done.11 = bf16[64,2048]{1,0:T(8,128)(2,1)S(1)} collective-permute-done((bf16[64,2048]{1,0:T(8,128)(2,1)S(1)}, bf16[64,2048]{1,0:T(8,128)(2,1)S(1)}, u32[]{:S(2)}, u32[]{:S(2)}) %collective-permute-start.11) | collective-permute-done | bytes 262176 | tf_op jit(solution)/shard_map/ppermute | solution.py:297
  40.4 0.7 %collective-permute-start.13 = (bf16[64,2048]{1,0:T(8,128)(2,1)S(1)}, bf16[64,2048]{1,0:T(8,128)(2,1)S(1)}, u32[]{:S(2)}, u32[]{:S(2)}) collective-permute-start(bf16[64,2048]{1,0:T(8,128)(2,1)S(1)} %add_convert_fusion.5), channel_id=1, source_target_pairs={{0,3},{1,4},{2,1},{3,6},{6,11},{7,2},{10,7},{11,14},{14,13},{15,10... | collective-permute-start | bytes 786440 | tf_op jit(solution)/shard_map/ppermute | solution.py:297
  41.1 2.1 %shard_map.72 = (f32[64,2048]{1,0:T(8,128)S(1)}, f32[64,2048]{1,0:T(8,128)S(1)}) custom-call(bf16[64,2176]{1,0:T(8,128)(2,1)S(1)} %collective-permute-done.3.refs_0_, bf16[64,2176]{1,0:T(8,128)(2,1)S(1)} %collective-permute-done.refs_1_, bf16[1,2048,768]{2,1,0:T(8,128)(2,1)S(1)} %collective-permute-done.7.refs_5_.refs_2_, ...), custom_call_target="tpu_custom_call" | custom-call | flops 1207959552 | bytes 10485760 | tf_op jit(solution)/shard_map/pallas_call | solution.py:141
  43.2 0.7 %collective-permute-done.10 = bf16[64,2048]{1,0:T(8,128)(2,1)S(1)} collective-permute-done((bf16[64,2048]{1,0:T(8,128)(2,1)S(1)}, bf16[64,2048]{1,0:T(8,128)(2,1)S(1)}, u32[]{:S(2)}, u32[]{:S(2)}) %collective-permute-start.10) | collective-permute-done | bytes 262176 | tf_op jit(solution)/shard_map/ppermute | solution.py:297
  43.8 0.1 add_convert_fusion.4
  43.9 0.7 %collective-permute-start.12 = (bf16[64,2048]{1,0:T(8,128)(2,1)S(1)}, bf16[64,2048]{1,0:T(8,128)(2,1)S(1)}, u32[]{:S(2)}, u32[]{:S(2)}) collective-permute-start(bf16[64,2048]{1,0:T(8,128)(2,1)S(1)} %add_convert_fusion.4), channel_id=1, source_target_pairs={{0,5},{1,2},{2,7},{3,0},{6,3},{7,10},{10,15},{11,6},{14,11},{15,12... | collective-permute-start | bytes 786440 | tf_op jit(solution)/shard_map/ppermute | solution.py:297
  44.6 2.6 %collective-permute-done.13 = bf16[64,2048]{1,0:T(8,128)(2,1)S(1)} collective-permute-done((bf16[64,2048]{1,0:T(8,128)(2,1)S(1)}, bf16[64,2048]{1,0:T(8,128)(2,1)S(1)}, u32[]{:S(2)}, u32[]{:S(2)}) %collective-permute-start.13) | collective-permute-done | bytes 262176 | tf_op jit(solution)/shard_map/ppermute | solution.py:297
  47.2 0.1 add_convert_fusion.3
  47.3 0.1 collective-permute-start.15
  47.3 2.1 %shard_map.73 = (f32[64,2048]{1,0:T(8,128)S(1)}, f32[64,2048]{1,0:T(8,128)S(1)}) custom-call(bf16[64,2176]{1,0:T(8,128)(2,1)S(1)} %collective-permute-done.1.refs_0_, bf16[64,2176]{1,0:T(8,128)(2,1)S(1)} %shard_map.64.rows_ref.refs_1_, bf16[1,2048,768]{2,1,0:T(8,128)(2,1)S(1)} %collective-permute-done.7.refs_5_.refs_2_, ...), custom_call_target="tpu_custom_call" | custom-call | flops 1207959552 | bytes 10485760 | tf_op jit(solution)/shard_map/pallas_call | solution.py:141
  49.4 0.6 %collective-permute-done.12 = bf16[64,2048]{1,0:T(8,128)(2,1)S(1)} collective-permute-done((bf16[64,2048]{1,0:T(8,128)(2,1)S(1)}, bf16[64,2048]{1,0:T(8,128)(2,1)S(1)}, u32[]{:S(2)}, u32[]{:S(2)}) %collective-permute-start.12) | collective-permute-done | bytes 262176 | tf_op jit(solution)/shard_map/ppermute | solution.py:297
  50.1 0.1 add_convert_fusion.2
  50.1 1.1 %collective-permute-start.14 = (bf16[64,2048]{1,0:T(8,128)(2,1)S(1)}, bf16[64,2048]{1,0:T(8,128)(2,1)S(1)}, u32[]{:S(2)}, u32[]{:S(2)}) collective-permute-start(bf16[64,2048]{1,0:T(8,128)(2,1)S(1)} %add_convert_fusion.2), channel_id=1, source_target_pairs={{0,5},{1,2},{2,7},{3,0},{6,3},{7,10},{10,15},{11,6},{14,11},{15,12... | collective-permute-start | bytes 786440 | tf_op jit(solution)/shard_map/ppermute | solution.py:297
  51.3 3.1 %collective-permute-done.15 = bf16[64,2048]{1,0:T(8,128)(2,1)S(1)} collective-permute-done((bf16[64,2048]{1,0:T(8,128)(2,1)S(1)}, bf16[64,2048]{1,0:T(8,128)(2,1)S(1)}, u32[]{:S(2)}, u32[]{:S(2)}) %collective-permute-start.15) | collective-permute-done | bytes 262176 | tf_op jit(solution)/shard_map/ppermute | solution.py:297
  54.4 0.1 collective-permute-start.16
  54.5 1.5 %collective-permute-done.14 = bf16[64,2048]{1,0:T(8,128)(2,1)S(1)} collective-permute-done((bf16[64,2048]{1,0:T(8,128)(2,1)S(1)}, bf16[64,2048]{1,0:T(8,128)(2,1)S(1)}, u32[]{:S(2)}, u32[]{:S(2)}) %collective-permute-start.14) | collective-permute-done | bytes 262176 | tf_op jit(solution)/shard_map/ppermute | solution.py:297
  56.0 0.1 convert_add_fusion
  56.1 5.7 %collective-permute-done.16 = bf16[64,2048]{1,0:T(8,128)(2,1)S(1)} collective-permute-done((bf16[64,2048]{1,0:T(8,128)(2,1)S(1)}, bf16[64,2048]{1,0:T(8,128)(2,1)S(1)}, u32[]{:S(2)}, u32[]{:S(2)}) %collective-permute-start.16) | collective-permute-done | bytes 262176 | tf_op jit(solution)/shard_map/ppermute | solution.py:297
  61.8 0.8 %add_convert_fusion = bf16[64,2048]{1,0:T(8,128)(2,1)} fusion(f32[64,2048]{1,0:T(8,128)S(1)} %convert_add_fusion, bf16[64,2048]{1,0:T(8,128)(2,1)S(1)} %collective-permute-done.16), kind=kLoop, calls=%fused_computation | loop fusion | flops 393216 | bytes 1048576 | tf_op jit(solution)/shard_map/convert_element_type | solution.py:275
  (4 shorter events, 0.2 us)
Async XLA Ops:
  0.0 31.4 %collective-permute-start.7 = (bf16[1,2048,768]{2,1,0:T(8,128)(2,1)}, bf16[1,2048,768]{2,1,0:T(8,128)(2,1)S(1)}, u32[]{:S(2)}, u32[]{:S(2)}) collective-permute-start(bf16[1,2048,768]{2,1,0:T(8,128)(2,1)} %gate_in.1), channel_id=1, source_target_pairs={{0,1},{1,0},{2,3},{3,2},{4,5},{5,4},{6,7},{7,6},{8,9},{9,8},{10,11... | collective-permute-start | bytes 9437192 | tf_op jit(solution)/shard_map/ppermute | solution.py:300
  0.5 31.0 %collective-permute-start.8 = (bf16[1,2048,768]{2,1,0:T(8,128)(2,1)}, bf16[1,2048,768]{2,1,0:T(8,128)(2,1)S(1)}, u32[]{:S(2)}, u32[]{:S(2)}) collective-permute-start(bf16[1,2048,768]{2,1,0:T(8,128)(2,1)} %up_in.1), channel_id=1, source_target_pairs={{0,1},{1,0},{2,3},{3,2},{4,5},{5,4},{6,7},{7,6},{8,9},{9,8},{10,11... | collective-permute-start | bytes 9437192 | tf_op jit(solution)/shard_map/ppermute | solution.py:300
  0.5 30.9 %collective-permute-start.9 = (bf16[1,768,2048]{2,1,0:T(8,128)(2,1)}, bf16[1,768,2048]{2,1,0:T(8,128)(2,1)S(1)}, u32[]{:S(2)}, u32[]{:S(2)}) collective-permute-start(bf16[1,768,2048]{2,1,0:T(8,128)(2,1)} %down_in.1), channel_id=1, source_target_pairs={{0,1},{1,0},{2,3},{3,2},{4,5},{5,4},{6,7},{7,6},{8,9},{9,8},{10,11... | collective-permute-start | bytes 9437192 | tf_op jit(solution)/shard_map/ppermute | solution.py:300
  2.0 8.3 %collective-permute-start.1 = (bf16[64,2176]{1,0:T(8,128)(2,1)S(1)}, bf16[64,2176]{1,0:T(8,128)(2,1)S(1)}, u32[]{:S(2)}, u32[]{:S(2)}) collective-permute-start(bf16[64,2176]{1,0:T(8,128)(2,1)S(1)} %shard_map.64.rows_ref.refs_1_), channel_id=1, source_target_pairs={{0,5},{1,2},{2,7},{3,0},{6,3},{7,10},{10,15},{11,6},{14,11},{15,12... | collective-permute-start | bytes 835592 | tf_op jit(solution)/shard_map/ppermute | solution.py:294
  8.0 6.5 %collective-permute-start = (bf16[64,2176]{1,0:T(8,128)(2,1)S(1)}, bf16[64,2176]{1,0:T(8,128)(2,1)S(1)}, u32[]{:S(2)}, u32[]{:S(2)}) collective-permute-start(bf16[64,2176]{1,0:T(8,128)(2,1)S(1)} %shard_map.64.rows_ref.refs_1_), channel_id=1, source_target_pairs={{0,3},{1,4},{2,1},{3,6},{6,11},{7,2},{10,7},{11,14},{14,13},{15,10... | collective-permute-start | bytes 835592 | tf_op jit(solution)/shard_map/ppermute | solution.py:294
  10.2 6.9 %collective-permute-start.3 = (bf16[64,2176]{1,0:T(8,128)(2,1)S(1)}, bf16[64,2176]{1,0:T(8,128)(2,1)S(1)}, u32[]{:S(2)}, u32[]{:S(2)}) collective-permute-start(bf16[64,2176]{1,0:T(8,128)(2,1)S(1)} %collective-permute-done.1.refs_0_), channel_id=1, source_target_pairs={{0,5},{1,2},{2,7},{3,0},{6,3},{7,10},{10,15},{11,6},{14,11},{15,12... | collective-permute-start | bytes 835592 | tf_op jit(solution)/shard_map/ppermute | solution.py:294
  14.5 6.5 %collective-permute-start.2 = (bf16[64,2176]{1,0:T(8,128)(2,1)S(1)}, bf16[64,2176]{1,0:T(8,128)(2,1)S(1)}, u32[]{:S(2)}, u32[]{:S(2)}) collective-permute-start(bf16[64,2176]{1,0:T(8,128)(2,1)S(1)} %collective-permute-done.refs_1_), channel_id=1, source_target_pairs={{0,3},{1,4},{2,1},{3,6},{6,11},{7,2},{10,7},{11,14},{14,13},{15,10... | collective-permute-start | bytes 835592 | tf_op jit(solution)/shard_map/ppermute | solution.py:294
  17.1 7.0 %collective-permute-start.5 = (bf16[64,2176]{1,0:T(8,128)(2,1)S(1)}, bf16[64,2176]{1,0:T(8,128)(2,1)S(1)}, u32[]{:S(2)}, u32[]{:S(2)}) collective-permute-start(bf16[64,2176]{1,0:T(8,128)(2,1)S(1)} %collective-permute-done.3.refs_0_), channel_id=1, source_target_pairs={{0,5},{1,2},{2,7},{3,0},{6,3},{7,10},{10,15},{11,6},{14,11},{15,12... | collective-permute-start | bytes 835592 | tf_op jit(solution)/shard_map/ppermute | solution.py:294
  21.0 7.2 %collective-permute-start.4 = (bf16[64,2176]{1,0:T(8,128)(2,1)S(1)}, bf16[64,2176]{1,0:T(8,128)(2,1)S(1)}, u32[]{:S(2)}, u32[]{:S(2)}) collective-permute-start(bf16[64,2176]{1,0:T(8,128)(2,1)S(1)} %collective-permute-done.2.refs_1_), channel_id=1, source_target_pairs={{0,3},{1,4},{2,1},{3,6},{6,11},{7,2},{10,7},{11,14},{14,13},{15,10... | collective-permute-start | bytes 835592 | tf_op jit(solution)/shard_map/ppermute | solution.py:294
  24.2 7.3 %collective-permute-start.6 = (bf16[64,2176]{1,0:T(8,128)(2,1)S(1)}, bf16[64,2176]{1,0:T(8,128)(2,1)S(1)}, u32[]{:S(2)}, u32[]{:S(2)}) collective-permute-start(bf16[64,2176]{1,0:T(8,128)(2,1)S(1)} %collective-permute-done.5.refs_0_), channel_id=1, source_target_pairs={{0,5},{1,2},{2,7},{3,0},{6,3},{7,10},{10,15},{11,6},{14,11},{15,12... | collective-permute-start | bytes 835592 | tf_op jit(solution)/shard_map/ppermute | solution.py:294
  34.3 6.0 %collective-permute-start.11 = (bf16[64,2048]{1,0:T(8,128)(2,1)S(1)}, bf16[64,2048]{1,0:T(8,128)(2,1)S(1)}, u32[]{:S(2)}, u32[]{:S(2)}) collective-permute-start(bf16[64,2048]{1,0:T(8,128)(2,1)S(1)} %convert_element_type.45), channel_id=1, source_target_pairs={{0,3},{1,4},{2,1},{3,6},{6,11},{7,2},{10,7},{11,14},{14,13},{15,10... | collective-permute-start | bytes 786440 | tf_op jit(solution)/shard_map/ppermute | solution.py:297
  36.9 6.9 %collective-permute-start.10 = (bf16[64,2048]{1,0:T(8,128)(2,1)S(1)}, bf16[64,2048]{1,0:T(8,128)(2,1)S(1)}, u32[]{:S(2)}, u32[]{:S(2)}) collective-permute-start(bf16[64,2048]{1,0:T(8,128)(2,1)S(1)} %convert_element_type.46), channel_id=1, source_target_pairs={{0,5},{1,2},{2,7},{3,0},{6,3},{7,10},{10,15},{11,6},{14,11},{15,12... | collective-permute-start | bytes 786440 | tf_op jit(solution)/shard_map/ppermute | solution.py:297
  40.4 6.9 %collective-permute-start.13 = (bf16[64,2048]{1,0:T(8,128)(2,1)S(1)}, bf16[64,2048]{1,0:T(8,128)(2,1)S(1)}, u32[]{:S(2)}, u32[]{:S(2)}) collective-permute-start(bf16[64,2048]{1,0:T(8,128)(2,1)S(1)} %add_convert_fusion.5), channel_id=1, source_target_pairs={{0,3},{1,4},{2,1},{3,6},{6,11},{7,2},{10,7},{11,14},{14,13},{15,10... | collective-permute-start | bytes 786440 | tf_op jit(solution)/shard_map/ppermute | solution.py:297
  43.9 6.2 %collective-permute-start.12 = (bf16[64,2048]{1,0:T(8,128)(2,1)S(1)}, bf16[64,2048]{1,0:T(8,128)(2,1)S(1)}, u32[]{:S(2)}, u32[]{:S(2)}) collective-permute-start(bf16[64,2048]{1,0:T(8,128)(2,1)S(1)} %add_convert_fusion.4), channel_id=1, source_target_pairs={{0,5},{1,2},{2,7},{3,0},{6,3},{7,10},{10,15},{11,6},{14,11},{15,12... | collective-permute-start | bytes 786440 | tf_op jit(solution)/shard_map/ppermute | solution.py:297
  47.3 7.1 %collective-permute-start.15 = (bf16[64,2048]{1,0:T(8,128)(2,1)S(1)}, bf16[64,2048]{1,0:T(8,128)(2,1)S(1)}, u32[]{:S(2)}, u32[]{:S(2)}) collective-permute-start(bf16[64,2048]{1,0:T(8,128)(2,1)S(1)} %add_convert_fusion.3), channel_id=1, source_target_pairs={{0,3},{1,4},{2,1},{3,6},{6,11},{7,2},{10,7},{11,14},{14,13},{15,10... | collective-permute-start | bytes 786440 | tf_op jit(solution)/shard_map/ppermute | solution.py:297
  50.1 5.9 %collective-permute-start.14 = (bf16[64,2048]{1,0:T(8,128)(2,1)S(1)}, bf16[64,2048]{1,0:T(8,128)(2,1)S(1)}, u32[]{:S(2)}, u32[]{:S(2)}) collective-permute-start(bf16[64,2048]{1,0:T(8,128)(2,1)S(1)} %add_convert_fusion.2), channel_id=1, source_target_pairs={{0,5},{1,2},{2,7},{3,0},{6,3},{7,10},{10,15},{11,6},{14,11},{15,12... | collective-permute-start | bytes 786440 | tf_op jit(solution)/shard_map/ppermute | solution.py:297
  54.4 7.3 %collective-permute-start.16 = (bf16[64,2048]{1,0:T(8,128)(2,1)S(1)}, bf16[64,2048]{1,0:T(8,128)(2,1)S(1)}, u32[]{:S(2)}, u32[]{:S(2)}) collective-permute-start(bf16[64,2048]{1,0:T(8,128)(2,1)S(1)} %add_convert_fusion.1), channel_id=1, source_target_pairs={{0,3},{1,4},{2,1},{3,6},{6,11},{7,2},{10,7},{11,14},{14,13},{15,10... | collective-permute-start | bytes 786440 | tf_op jit(solution)/shard_map/ppermute | solution.py:297

commit v3 on v0

--- a/solution.py
+++ b/solution.py
@@ -297,7 +297,8 @@
         return lax.ppermute(block, "expert", ways[1 - way])
 
     first = pack_rows(tokens, expert_ids, gate_weights, made)
-    other = tuple(lax.ppermute(array, "expert", siblings) for array in own)
+    first, ready = after((first, own))
+    other = tuple(lax.ppermute(array, "expert", siblings) for array in ready)
 
     rows = {(0, 0): first}
     partial = {}

time: 62.2 us -> 62.1 us (level)
    ppermute x7, waiting for transfers between devices: 15.6 us -> 14.7 us  [homeward(): return lax.ppermute(block, 'expert', ways[1 - way])]
    ppermute x7, waiting for transfers between devices: 10.9 us -> 11.6 us  [outward(): return lax.ppermute(block, 'expert', ways[way])]
  transfers between devices with their start and end apart: 17 -> 17, of which waited for: 12 -> 13; matrix products, arithmetic and copies ran while one was open for 1% -> 1% of each run, Pallas kernels for 30% -> 29%
where the time goes in v3:
time: 62.1 us; the launch traced here: 61.7 us
  waiting for transfers between devices  26.2 us (42%)
  Pallas kernels  21.6 us (35%)
  starting transfers between devices  12.6 us (20%)
  other arithmetic  1.15 us (2%)
    pallas_call x7, Pallas kernels, run_experts(): pl.pallas_call(functools.partial(expert_kernel, blocks, flips, bool(prior...  15.1 us
    ppermute x7, waiting for transfers between devices, homeward(): return lax.ppermute(block, 'expert', ways[1 - way])  14.7 us
    ppermute x7, waiting for transfers between devices, outward(): return lax.ppermute(block, 'expert', ways[way])  11.6 us
    ppermute x7, starting transfers between devices, outward(): return lax.ppermute(block, 'expert', ways[way])  6.59 us
    ppermute x7, starting transfers between devices, homeward(): return lax.ppermute(block, 'expert', ways[1 - way])  5 us
    pallas_call x1, Pallas kernels, take_inputs_in(): pl.pallas_call(first_kernel, out_shape=[made((rows, hidden_width), jnp.bf...  3.25 us
    pallas_call x1, Pallas kernels, take_output_in(): pl.pallas_call(functools.partial(second_kernel, top_count), out_shape=[ma...  2.18 us
  transfers between devices with their start and end apart: 17, of which 13 were waited for; matrix products, arithmetic and copies ran while one was open for 1% of the time, Pallas kernels for 29%

profile of v3, /device:TPU:0, one launch (start us, length us, event | category | flops | bytes accessed | tf_op | source)
XLA Modules:
  0.0 61.7 jit_solution(16494673205995708644)
XLA Ops:
  0.0 1.0 %shard_map.64.rows_ref.refs_1_ = bf16[64,2176]{1,0:T(8,128)(2,1)S(1)} custom-call(bf16[64,2048]{1,0:T(8,128)(2,1)} %tokens_ref.1, s32[8,64]{1,0:T(8,128)} %bitcast.2, f32[8,64]{1,0:T(8,128)} %bitcast.3), custom_call_target="tpu_custom_call" | custom-call | tf_op jit(solution)/shard_map/pallas_call | solution.py:86
  1.0 0.5 collective-permute-start.7
  1.5 0.1 collective-permute-start.8
  1.6 0.4 collective-permute-start.9
  2.0 2.6 %collective-permute-start.1 = (bf16[64,2176]{1,0:T(8,128)(2,1)S(1)}, bf16[64,2176]{1,0:T(8,128)(2,1)S(1)}, u32[]{:S(2)}, u32[]{:S(2)}) collective-permute-start(bf16[64,2176]{1,0:T(8,128)(2,1)S(1)} %shard_map.64.rows_ref.refs_1_), channel_id=1, source_target_pairs={{0,3},{1,4},{2,1},{3,6},{6,11},{7,2},{10,7},{11,14},{14,13},{15,10... | collective-permute-start | bytes 835592 | tf_op jit(solution)/shard_map/ppermute | solution.py:294
  4.7 3.2 %shard_map.65 = (bf16[64,768]{1,0:T(8,128)(2,1)S(1)}, bf16[1,2048,768]{2,1,0:T(8,128)(2,1)S(1)}, bf16[1,2048,768]{2,1,0:T(8,128)(2,1)S(1)}) custom-call(bf16[64,2176]{1,0:T(8,128)(2,1)S(1)} %shard_map.64.rows_ref.refs_1_, bf16[1,2048,768]{2,1,0:T(8,128)(2,1)} %gate_in.1, bf16[1,2048,768]{2,1,0:T(8,128)(2,1)} %up_in.1), custom_call_target="tpu_custom_call" | custom-call | flops 402653184 | bytes 6291456 | tf_op jit(solution)/shard_map/pallas_call | solution.py:219
  7.9 0.1 collective-permute-start
  8.0 2.2 %shard_map.66 = (f32[64,2048]{1,0:T(8,128)S(1)}, bf16[1,768,2048]{2,1,0:T(8,128)(2,1)S(1)}) custom-call(bf16[64,2176]{1,0:T(8,128)(2,1)S(1)} %shard_map.64.rows_ref.refs_1_, bf16[64,768]{1,0:T(8,128)(2,1)S(1)} %get-tuple-element.58.hidden_ref, bf16[1,768,2048]{2,1,0:T(8,128)(2,1)} %down_in.1), custom_call_target="tpu_custom_call" | custom-call | flops 201326592 | bytes 3145728 | tf_op jit(solution)/shard_map/pallas_call | solution.py:241
  10.2 0.0 collective-permute-done.1.refs_0_
  10.2 1.7 %collective-permute-start.3 = (bf16[64,2176]{1,0:T(8,128)(2,1)S(1)}, bf16[64,2176]{1,0:T(8,128)(2,1)S(1)}, u32[]{:S(2)}, u32[]{:S(2)}) collective-permute-start(bf16[64,2176]{1,0:T(8,128)(2,1)S(1)} %collective-permute-done.1.refs_0_), channel_id=1, source_target_pairs={{0,3},{1,4},{2,1},{3,6},{6,11},{7,2},{10,7},{11,14},{14,13},{15,10... | collective-permute-start | bytes 835592 | tf_op jit(solution)/shard_map/ppermute | solution.py:294
  12.0 2.0 %shard_map.67.refs_5_ = f32[64,2048]{1,0:T(8,128)S(1)} custom-call(bf16[64,2176]{1,0:T(8,128)(2,1)S(1)} %collective-permute-done.1.refs_0_, bf16[1,2048,768]{2,1,0:T(8,128)(2,1)S(1)} %get-tuple-element.61.refs_1_.refs_2_, bf16[1,2048,768]{2,1,0:T(8,128)(2,1)S(1)} %get-tuple-element.62.refs_2_.refs_3_, bf16[1,768,2048]{2,1,0:T(8,128)(2,1)S(1)} %get-tuple-element.63.refs_3_.refs_4_), custom_call_target="tpu_custom_call" | custom-call | flops 603979776 | bytes 9961472 | tf_op jit(solution)/shard_map/pallas_call | solution.py:141
  14.0 0.2 collective-permute-done.refs_1_
  14.3 0.0 collective-permute-start.2
  14.3 2.9 %collective-permute-done.3.refs_0_ = bf16[64,2176]{1,0:T(8,128)(2,1)S(1)} collective-permute-done((bf16[64,2176]{1,0:T(8,128)(2,1)S(1)}, bf16[64,2176]{1,0:T(8,128)(2,1)S(1)}, u32[]{:S(2)}, u32[]{:S(2)}) %collective-permute-start.3) | collective-permute-done | bytes 278560 | tf_op jit(solution)/shard_map/ppermute | solution.py:294
  17.3 1.3 %collective-permute-start.5 = (bf16[64,2176]{1,0:T(8,128)(2,1)S(1)}, bf16[64,2176]{1,0:T(8,128)(2,1)S(1)}, u32[]{:S(2)}, u32[]{:S(2)}) collective-permute-start(bf16[64,2176]{1,0:T(8,128)(2,1)S(1)} %collective-permute-done.3.refs_0_), channel_id=1, source_target_pairs={{0,3},{1,4},{2,1},{3,6},{6,11},{7,2},{10,7},{11,14},{14,13},{15,10... | collective-permute-start | bytes 835592 | tf_op jit(solution)/shard_map/ppermute | solution.py:294
  18.5 2.0 %shard_map.68 = (f32[64,2048]{1,0:T(8,128)S(1)}, f32[64,2048]{1,0:T(8,128)S(1)}) custom-call(bf16[64,2176]{1,0:T(8,128)(2,1)S(1)} %collective-permute-done.3.refs_0_, bf16[64,2176]{1,0:T(8,128)(2,1)S(1)} %collective-permute-done.refs_1_, bf16[1,2048,768]{2,1,0:T(8,128)(2,1)S(1)} %get-tuple-element.61.refs_1_.refs_2_, ...), custom_call_target="tpu_custom_call" | custom-call | flops 1207959552 | bytes 10485760 | tf_op jit(solution)/shard_map/pallas_call | solution.py:141
  20.6 0.1 collective-permute-done.2.refs_1_
  20.7 0.5 collective-permute-start.4
  21.1 3.3 %collective-permute-done.5.refs_0_ = bf16[64,2176]{1,0:T(8,128)(2,1)S(1)} collective-permute-done((bf16[64,2176]{1,0:T(8,128)(2,1)S(1)}, bf16[64,2176]{1,0:T(8,128)(2,1)S(1)}, u32[]{:S(2)}, u32[]{:S(2)}) %collective-permute-start.5) | collective-permute-done | bytes 278560 | tf_op jit(solution)/shard_map/ppermute | solution.py:294
  24.4 0.4 collective-permute-start.6
  24.8 2.1 %shard_map.69 = (f32[64,2048]{1,0:T(8,128)S(1)}, f32[64,2048]{1,0:T(8,128)S(1)}) custom-call(bf16[64,2176]{1,0:T(8,128)(2,1)S(1)} %collective-permute-done.5.refs_0_, bf16[64,2176]{1,0:T(8,128)(2,1)S(1)} %collective-permute-done.2.refs_1_, bf16[1,2048,768]{2,1,0:T(8,128)(2,1)S(1)} %get-tuple-element.61.refs_1_.refs_2_, ...), custom_call_target="tpu_custom_call" | custom-call | flops 1207959552 | bytes 10485760 | tf_op jit(solution)/shard_map/pallas_call | solution.py:141
  26.9 1.3 %collective-permute-done.4.refs_0_ = bf16[64,2176]{1,0:T(8,128)(2,1)S(1)} collective-permute-done((bf16[64,2176]{1,0:T(8,128)(2,1)S(1)}, bf16[64,2176]{1,0:T(8,128)(2,1)S(1)}, u32[]{:S(2)}, u32[]{:S(2)}) %collective-permute-start.4) | collective-permute-done | bytes 278560 | tf_op jit(solution)/shard_map/ppermute | solution.py:294
  28.2 3.7 %collective-permute-done.6.refs_1_ = bf16[64,2176]{1,0:T(8,128)(2,1)S(1)} collective-permute-done((bf16[64,2176]{1,0:T(8,128)(2,1)S(1)}, bf16[64,2176]{1,0:T(8,128)(2,1)S(1)}, u32[]{:S(2)}, u32[]{:S(2)}) %collective-permute-start.6) | collective-permute-done | bytes 278560 | tf_op jit(solution)/shard_map/ppermute | solution.py:294
  31.8 0.0 collective-permute-done.7.refs_5_.refs_2_
  31.9 0.0 collective-permute-done.8.refs_6_.refs_3_
  31.9 0.0 collective-permute-done.9.refs_7_.refs_4_
  31.9 2.8 %shard_map.70 = (f32[64,2048]{1,0:T(8,128)S(1)}, f32[64,2048]{1,0:T(8,128)S(1)}) custom-call(bf16[64,2176]{1,0:T(8,128)(2,1)S(1)} %collective-permute-done.4.refs_0_, bf16[64,2176]{1,0:T(8,128)(2,1)S(1)} %collective-permute-done.6.refs_1_, bf16[1,2048,768]{2,1,0:T(8,128)(2,1)S(1)} %get-tuple-element.61.refs_1_.refs_2_, ...), custom_call_target="tpu_custom_call" | custom-call | flops 2415919104 | bytes 19922944 | tf_op jit(solution)/shard_map/pallas_call | solution.py:141
  34.7 0.2 collective-permute-start.11
  35.0 2.1 %shard_map.71 = (f32[64,2048]{1,0:T(8,128)S(1)}, f32[64,2048]{1,0:T(8,128)S(1)}) custom-call(bf16[64,2176]{1,0:T(8,128)(2,1)S(1)} %collective-permute-done.5.refs_0_, bf16[64,2176]{1,0:T(8,128)(2,1)S(1)} %collective-permute-done.2.refs_1_, bf16[1,2048,768]{2,1,0:T(8,128)(2,1)S(1)} %collective-permute-done.7.refs_5_.refs_2_, ...), custom_call_target="tpu_custom_call" | custom-call | flops 1207959552 | bytes 10485760 | tf_op jit(solution)/shard_map/pallas_call | solution.py:141
  37.1 1.8 %collective-permute-start.10 = (bf16[64,2048]{1,0:T(8,128)(2,1)S(1)}, bf16[64,2048]{1,0:T(8,128)(2,1)S(1)}, u32[]{:S(2)}, u32[]{:S(2)}) collective-permute-start(bf16[64,2048]{1,0:T(8,128)(2,1)S(1)} %convert_element_type.46), channel_id=1, source_target_pairs={{0,3},{1,4},{2,1},{3,6},{6,11},{7,2},{10,7},{11,14},{14,13},{15,10... | collective-permute-start | bytes 786440 | tf_op jit(solution)/shard_map/ppermute | solution.py:297
  38.8 1.9 %collective-permute-done.11 = bf16[64,2048]{1,0:T(8,128)(2,1)S(1)} collective-permute-done((bf16[64,2048]{1,0:T(8,128)(2,1)S(1)}, bf16[64,2048]{1,0:T(8,128)(2,1)S(1)}, u32[]{:S(2)}, u32[]{:S(2)}) %collective-permute-start.11) | collective-permute-done | bytes 262176 | tf_op jit(solution)/shard_map/ppermute | solution.py:297
  40.8 0.5 collective-permute-start.13
  41.2 2.1 %shard_map.72 = (f32[64,2048]{1,0:T(8,128)S(1)}, f32[64,2048]{1,0:T(8,128)S(1)}) custom-call(bf16[64,2176]{1,0:T(8,128)(2,1)S(1)} %collective-permute-done.3.refs_0_, bf16[64,2176]{1,0:T(8,128)(2,1)S(1)} %collective-permute-done.refs_1_, bf16[1,2048,768]{2,1,0:T(8,128)(2,1)S(1)} %collective-permute-done.7.refs_5_.refs_2_, ...), custom_call_target="tpu_custom_call" | custom-call | flops 1207959552 | bytes 10485760 | tf_op jit(solution)/shard_map/pallas_call | solution.py:141
  43.3 0.8 %collective-permute-done.10 = bf16[64,2048]{1,0:T(8,128)(2,1)S(1)} collective-permute-done((bf16[64,2048]{1,0:T(8,128)(2,1)S(1)}, bf16[64,2048]{1,0:T(8,128)(2,1)S(1)}, u32[]{:S(2)}, u32[]{:S(2)}) %collective-permute-start.10) | collective-permute-done | bytes 262176 | tf_op jit(solution)/shard_map/ppermute | solution.py:297
  44.1 0.1 add_convert_fusion.4
  44.2 0.9 %collective-permute-start.12 = (bf16[64,2048]{1,0:T(8,128)(2,1)S(1)}, bf16[64,2048]{1,0:T(8,128)(2,1)S(1)}, u32[]{:S(2)}, u32[]{:S(2)}) collective-permute-start(bf16[64,2048]{1,0:T(8,128)(2,1)S(1)} %add_convert_fusion.4), channel_id=1, source_target_pairs={{0,3},{1,4},{2,1},{3,6},{6,11},{7,2},{10,7},{11,14},{14,13},{15,10... | collective-permute-start | bytes 786440 | tf_op jit(solution)/shard_map/ppermute | solution.py:297
  45.1 2.1 %collective-permute-done.13 = bf16[64,2048]{1,0:T(8,128)(2,1)S(1)} collective-permute-done((bf16[64,2048]{1,0:T(8,128)(2,1)S(1)}, bf16[64,2048]{1,0:T(8,128)(2,1)S(1)}, u32[]{:S(2)}, u32[]{:S(2)}) %collective-permute-start.13) | collective-permute-done | bytes 262176 | tf_op jit(solution)/shard_map/ppermute | solution.py:297
  47.3 0.1 add_convert_fusion.3
  47.3 0.1 collective-permute-start.15
  47.5 2.1 %shard_map.73 = (f32[64,2048]{1,0:T(8,128)S(1)}, f32[64,2048]{1,0:T(8,128)S(1)}) custom-call(bf16[64,2176]{1,0:T(8,128)(2,1)S(1)} %collective-permute-done.1.refs_0_, bf16[64,2176]{1,0:T(8,128)(2,1)S(1)} %shard_map.64.rows_ref.refs_1_, bf16[1,2048,768]{2,1,0:T(8,128)(2,1)S(1)} %collective-permute-done.7.refs_5_.refs_2_, ...), custom_call_target="tpu_custom_call" | custom-call | flops 1207959552 | bytes 10485760 | tf_op jit(solution)/shard_map/pallas_call | solution.py:141
  49.5 0.6 collective-permute-done.12
  50.1 0.1 add_convert_fusion.2
  50.2 1.4 %collective-permute-start.14 = (bf16[64,2048]{1,0:T(8,128)(2,1)S(1)}, bf16[64,2048]{1,0:T(8,128)(2,1)S(1)}, u32[]{:S(2)}, u32[]{:S(2)}) collective-permute-start(bf16[64,2048]{1,0:T(8,128)(2,1)S(1)} %add_convert_fusion.2), channel_id=1, source_target_pairs={{0,3},{1,4},{2,1},{3,6},{6,11},{7,2},{10,7},{11,14},{14,13},{15,10... | collective-permute-start | bytes 786440 | tf_op jit(solution)/shard_map/ppermute | solution.py:297
  51.6 2.4 %collective-permute-done.15 = bf16[64,2048]{1,0:T(8,128)(2,1)S(1)} collective-permute-done((bf16[64,2048]{1,0:T(8,128)(2,1)S(1)}, bf16[64,2048]{1,0:T(8,128)(2,1)S(1)}, u32[]{:S(2)}, u32[]{:S(2)}) %collective-permute-start.15) | collective-permute-done | bytes 262176 | tf_op jit(solution)/shard_map/ppermute | solution.py:297
  54.1 0.1 collective-permute-start.16
  54.1 2.0 %collective-permute-done.14 = bf16[64,2048]{1,0:T(8,128)(2,1)S(1)} collective-permute-done((bf16[64,2048]{1,0:T(8,128)(2,1)S(1)}, bf16[64,2048]{1,0:T(8,128)(2,1)S(1)}, u32[]{:S(2)}, u32[]{:S(2)}) %collective-permute-start.14) | collective-permute-done | bytes 262176 | tf_op jit(solution)/shard_map/ppermute | solution.py:297
  56.2 0.1 convert_add_fusion
  56.2 4.8 %collective-permute-done.16 = bf16[64,2048]{1,0:T(8,128)(2,1)S(1)} collective-permute-done((bf16[64,2048]{1,0:T(8,128)(2,1)S(1)}, bf16[64,2048]{1,0:T(8,128)(2,1)S(1)}, u32[]{:S(2)}, u32[]{:S(2)}) %collective-permute-start.16) | collective-permute-done | bytes 262176 | tf_op jit(solution)/shard_map/ppermute | solution.py:297
  61.0 0.8 %add_convert_fusion = bf16[64,2048]{1,0:T(8,128)(2,1)} fusion(f32[64,2048]{1,0:T(8,128)S(1)} %convert_add_fusion, bf16[64,2048]{1,0:T(8,128)(2,1)S(1)} %collective-permute-done.16), kind=kLoop, calls=%fused_computation | loop fusion | flops 393216 | bytes 1048576 | tf_op jit(solution)/shard_map/convert_element_type | solution.py:275
  (4 shorter events, 0.2 us)
Async XLA Ops:
  1.0 30.8 %collective-permute-start.7 = (bf16[1,2048,768]{2,1,0:T(8,128)(2,1)}, bf16[1,2048,768]{2,1,0:T(8,128)(2,1)S(1)}, u32[]{:S(2)}, u32[]{:S(2)}) collective-permute-start(bf16[1,2048,768]{2,1,0:T(8,128)(2,1)} %gate_in.1), channel_id=1, source_target_pairs={{0,1},{1,0},{2,3},{3,2},{4,5},{5,4},{6,7},{7,6},{8,9},{9,8},{10,11... | collective-permute-start | bytes 9437192 | tf_op jit(solution)/shard_map/ppermute | solution.py:301
  1.5 30.3 %collective-permute-start.8 = (bf16[1,2048,768]{2,1,0:T(8,128)(2,1)}, bf16[1,2048,768]{2,1,0:T(8,128)(2,1)S(1)}, u32[]{:S(2)}, u32[]{:S(2)}) collective-permute-start(bf16[1,2048,768]{2,1,0:T(8,128)(2,1)} %up_in.1), channel_id=1, source_target_pairs={{0,1},{1,0},{2,3},{3,2},{4,5},{5,4},{6,7},{7,6},{8,9},{9,8},{10,11... | collective-permute-start | bytes 9437192 | tf_op jit(solution)/shard_map/ppermute | solution.py:301
  1.6 30.2 %collective-permute-start.9 = (bf16[1,768,2048]{2,1,0:T(8,128)(2,1)}, bf16[1,768,2048]{2,1,0:T(8,128)(2,1)S(1)}, u32[]{:S(2)}, u32[]{:S(2)}) collective-permute-start(bf16[1,768,2048]{2,1,0:T(8,128)(2,1)} %down_in.1), channel_id=1, source_target_pairs={{0,1},{1,0},{2,3},{3,2},{4,5},{5,4},{6,7},{7,6},{8,9},{9,8},{10,11... | collective-permute-start | bytes 9437192 | tf_op jit(solution)/shard_map/ppermute | solution.py:301
  2.0 8.2 %collective-permute-start.1 = (bf16[64,2176]{1,0:T(8,128)(2,1)S(1)}, bf16[64,2176]{1,0:T(8,128)(2,1)S(1)}, u32[]{:S(2)}, u32[]{:S(2)}) collective-permute-start(bf16[64,2176]{1,0:T(8,128)(2,1)S(1)} %shard_map.64.rows_ref.refs_1_), channel_id=1, source_target_pairs={{0,3},{1,4},{2,1},{3,6},{6,11},{7,2},{10,7},{11,14},{14,13},{15,10... | collective-permute-start | bytes 835592 | tf_op jit(solution)/shard_map/ppermute | solution.py:294
  7.9 6.4 %collective-permute-start = (bf16[64,2176]{1,0:T(8,128)(2,1)S(1)}, bf16[64,2176]{1,0:T(8,128)(2,1)S(1)}, u32[]{:S(2)}, u32[]{:S(2)}) collective-permute-start(bf16[64,2176]{1,0:T(8,128)(2,1)S(1)} %shard_map.64.rows_ref.refs_1_), channel_id=1, source_target_pairs={{0,5},{1,2},{2,7},{3,0},{6,3},{7,10},{10,15},{11,6},{14,11},{15,12... | collective-permute-start | bytes 835592 | tf_op jit(solution)/shard_map/ppermute | solution.py:294
  10.2 7.0 %collective-permute-start.3 = (bf16[64,2176]{1,0:T(8,128)(2,1)S(1)}, bf16[64,2176]{1,0:T(8,128)(2,1)S(1)}, u32[]{:S(2)}, u32[]{:S(2)}) collective-permute-start(bf16[64,2176]{1,0:T(8,128)(2,1)S(1)} %collective-permute-done.1.refs_0_), channel_id=1, source_target_pairs={{0,3},{1,4},{2,1},{3,6},{6,11},{7,2},{10,7},{11,14},{14,13},{15,10... | collective-permute-start | bytes 835592 | tf_op jit(solution)/shard_map/ppermute | solution.py:294
  14.3 6.4 %collective-permute-start.2 = (bf16[64,2176]{1,0:T(8,128)(2,1)S(1)}, bf16[64,2176]{1,0:T(8,128)(2,1)S(1)}, u32[]{:S(2)}, u32[]{:S(2)}) collective-permute-start(bf16[64,2176]{1,0:T(8,128)(2,1)S(1)} %collective-permute-done.refs_1_), channel_id=1, source_target_pairs={{0,5},{1,2},{2,7},{3,0},{6,3},{7,10},{10,15},{11,6},{14,11},{15,12... | collective-permute-start | bytes 835592 | tf_op jit(solution)/shard_map/ppermute | solution.py:294
  17.3 7.2 %collective-permute-start.5 = (bf16[64,2176]{1,0:T(8,128)(2,1)S(1)}, bf16[64,2176]{1,0:T(8,128)(2,1)S(1)}, u32[]{:S(2)}, u32[]{:S(2)}) collective-permute-start(bf16[64,2176]{1,0:T(8,128)(2,1)S(1)} %collective-permute-done.3.refs_0_), channel_id=1, source_target_pairs={{0,3},{1,4},{2,1},{3,6},{6,11},{7,2},{10,7},{11,14},{14,13},{15,10... | collective-permute-start | bytes 835592 | tf_op jit(solution)/shard_map/ppermute | solution.py:294
  20.7 7.5 %collective-permute-start.4 = (bf16[64,2176]{1,0:T(8,128)(2,1)S(1)}, bf16[64,2176]{1,0:T(8,128)(2,1)S(1)}, u32[]{:S(2)}, u32[]{:S(2)}) collective-permute-start(bf16[64,2176]{1,0:T(8,128)(2,1)S(1)} %collective-permute-done.2.refs_1_), channel_id=1, source_target_pairs={{0,5},{1,2},{2,7},{3,0},{6,3},{7,10},{10,15},{11,6},{14,11},{15,12... | collective-permute-start | bytes 835592 | tf_op jit(solution)/shard_map/ppermute | solution.py:294
  24.4 7.4 %collective-permute-start.6 = (bf16[64,2176]{1,0:T(8,128)(2,1)S(1)}, bf16[64,2176]{1,0:T(8,128)(2,1)S(1)}, u32[]{:S(2)}, u32[]{:S(2)}) collective-permute-start(bf16[64,2176]{1,0:T(8,128)(2,1)S(1)} %collective-permute-done.5.refs_0_), channel_id=1, source_target_pairs={{0,3},{1,4},{2,1},{3,6},{6,11},{7,2},{10,7},{11,14},{14,13},{15,10... | collective-permute-start | bytes 835592 | tf_op jit(solution)/shard_map/ppermute | solution.py:294
  34.7 6.0 %collective-permute-start.11 = (bf16[64,2048]{1,0:T(8,128)(2,1)S(1)}, bf16[64,2048]{1,0:T(8,128)(2,1)S(1)}, u32[]{:S(2)}, u32[]{:S(2)}) collective-permute-start(bf16[64,2048]{1,0:T(8,128)(2,1)S(1)} %convert_element_type.45), channel_id=1, source_target_pairs={{0,5},{1,2},{2,7},{3,0},{6,3},{7,10},{10,15},{11,6},{14,11},{15,12... | collective-permute-start | bytes 786440 | tf_op jit(solution)/shard_map/ppermute | solution.py:297
  37.1 7.0 %collective-permute-start.10 = (bf16[64,2048]{1,0:T(8,128)(2,1)S(1)}, bf16[64,2048]{1,0:T(8,128)(2,1)S(1)}, u32[]{:S(2)}, u32[]{:S(2)}) collective-permute-start(bf16[64,2048]{1,0:T(8,128)(2,1)S(1)} %convert_element_type.46), channel_id=1, source_target_pairs={{0,3},{1,4},{2,1},{3,6},{6,11},{7,2},{10,7},{11,14},{14,13},{15,10... | collective-permute-start | bytes 786440 | tf_op jit(solution)/shard_map/ppermute | solution.py:297
  40.8 6.5 %collective-permute-start.13 = (bf16[64,2048]{1,0:T(8,128)(2,1)S(1)}, bf16[64,2048]{1,0:T(8,128)(2,1)S(1)}, u32[]{:S(2)}, u32[]{:S(2)}) collective-permute-start(bf16[64,2048]{1,0:T(8,128)(2,1)S(1)} %add_convert_fusion.5), channel_id=1, source_target_pairs={{0,5},{1,2},{2,7},{3,0},{6,3},{7,10},{10,15},{11,6},{14,11},{15,12... | collective-permute-start | bytes 786440 | tf_op jit(solution)/shard_map/ppermute | solution.py:297
  44.2 6.0 %collective-permute-start.12 = (bf16[64,2048]{1,0:T(8,128)(2,1)S(1)}, bf16[64,2048]{1,0:T(8,128)(2,1)S(1)}, u32[]{:S(2)}, u32[]{:S(2)}) collective-permute-start(bf16[64,2048]{1,0:T(8,128)(2,1)S(1)} %add_convert_fusion.4), channel_id=1, source_target_pairs={{0,3},{1,4},{2,1},{3,6},{6,11},{7,2},{10,7},{11,14},{14,13},{15,10... | collective-permute-start | bytes 786440 | tf_op jit(solution)/shard_map/ppermute | solution.py:297
  47.3 6.7 %collective-permute-start.15 = (bf16[64,2048]{1,0:T(8,128)(2,1)S(1)}, bf16[64,2048]{1,0:T(8,128)(2,1)S(1)}, u32[]{:S(2)}, u32[]{:S(2)}) collective-permute-start(bf16[64,2048]{1,0:T(8,128)(2,1)S(1)} %add_convert_fusion.3), channel_id=1, source_target_pairs={{0,5},{1,2},{2,7},{3,0},{6,3},{7,10},{10,15},{11,6},{14,11},{15,12... | collective-permute-start | bytes 786440 | tf_op jit(solution)/shard_map/ppermute | solution.py:297
  50.2 6.0 %collective-permute-start.14 = (bf16[64,2048]{1,0:T(8,128)(2,1)S(1)}, bf16[64,2048]{1,0:T(8,128)(2,1)S(1)}, u32[]{:S(2)}, u32[]{:S(2)}) collective-permute-start(bf16[64,2048]{1,0:T(8,128)(2,1)S(1)} %add_convert_fusion.2), channel_id=1, source_target_pairs={{0,3},{1,4},{2,1},{3,6},{6,11},{7,2},{10,7},{11,14},{14,13},{15,10... | collective-permute-start | bytes 786440 | tf_op jit(solution)/shard_map/ppermute | solution.py:297
  54.1 6.9 %collective-permute-start.16 = (bf16[64,2048]{1,0:T(8,128)(2,1)S(1)}, bf16[64,2048]{1,0:T(8,128)(2,1)S(1)}, u32[]{:S(2)}, u32[]{:S(2)}) collective-permute-start(bf16[64,2048]{1,0:T(8,128)(2,1)S(1)} %add_convert_fusion.1), channel_id=1, source_target_pairs={{0,5},{1,2},{2,7},{3,0},{6,3},{7,10},{10,15},{11,6},{14,11},{15,12... | collective-permute-start | bytes 786440 | tf_op jit(solution)/shard_map/ppermute | solution.py:297
